TPU v7x, 512 devices: a whole 4x8x8 slice. The times are simulated.
512 devices in a mesh: dp: 64 (over x, y, z_hi), mp: 8 (over z_lo, core).
Axes of the slice: x: 4, y: 8, z: 8 (z_hi: 2, z_lo: 4; z = z_hi * 4 + z_lo), core: 2. Of those that a mesh axis runs over, the one named last changes fastest.
Arguments:
- layer_input: bfloat16 [32768, 1280], P('dp', 'mp'), may hold values from -6 to 6
- first_weight: bfloat16 [1280, 5120], P(None, 'mp'), may hold values from -0.15625 to 0.15625
- first_bias: float32 [5120], P('mp'), may hold values from -3 to 3
- hidden_grad: bfloat16 [32768, 5120], P('dp', 'mp'), may hold values from -51 to 51
- other_squares: float32 [128], P('dp'), may hold values from 0.05 to 1
- weight_noise: float32 [1280, 5120], P('dp', 'mp'), may hold values from -96 to 96
- bias_noise: float32 [5120], P('mp'), may hold values from -96 to 96
Outputs:
- input_grad: bfloat16 [32768, 1280], P('dp', 'mp')
- weight_grad: float32 [1280, 5120], P('dp', 'mp')
- bias_grad: float32 [5120], P('mp')
All inputs are finite; a program needn't handle non-finite values.
Results may differ from a plain program's by a relative error of at most 0.017.
Values may be sent and summed in bfloat16 or wider, within the bound.
A program may use at most 64 MiB of HBM per device.

v0:
```python
import math

import jax
import jax.numpy as jnp
from jax import lax
from jax.sharding import PartitionSpec as P

D = 1280
FF = 5120
SEQ = 256


def gelu_slope(pre_act):
    normal_cdf = 0.5 * (1.0 + lax.erf(pre_act * 0.7071067811865476))
    normal_pdf = jnp.exp(-0.5 * pre_act * pre_act) * 0.3989422804014327
    return normal_cdf + pre_act * normal_pdf


def per_device(
    layer_input, first_weight, first_bias, hidden_grad, other_squares, weight_noise, bias_noise
):
    gathered = lax.all_gather(layer_input, "mp", axis=1, tiled=True)
    pre_act = jnp.dot(gathered, first_weight, preferred_element_type=jnp.float32) + first_bias
    pre_grad = (hidden_grad.astype(jnp.float32) * gelu_slope(pre_act)).astype(jnp.bfloat16)
    back_terms = lax.dot_general(
        pre_grad, first_weight, (((1,), (1,)), ((), ())), preferred_element_type=jnp.float32
    )
    input_grad = lax.psum_scatter(
        back_terms.astype(jnp.bfloat16), "mp", scatter_dimension=1, tiled=True
    )
    local_count = hidden_grad.shape[0] // SEQ
    input_blocks = gathered.reshape(local_count, SEQ, gathered.shape[1])
    grad_blocks = pre_grad.reshape(local_count, SEQ, pre_grad.shape[1])
    per_grad = jnp.einsum(
        "bsd,bsf->bdf", input_blocks, grad_blocks, preferred_element_type=jnp.float32
    )
    bias_rows = jnp.sum(grad_blocks.astype(jnp.float32), axis=1)
    input_gram = jnp.einsum(
        "bsd,btd->bst", input_blocks, input_blocks, preferred_element_type=jnp.float32
    )
    grad_gram = jnp.einsum(
        "bsf,btf->bst", grad_blocks, grad_blocks, preferred_element_type=jnp.float32
    )
    partial_value = jnp.sum(input_gram * grad_gram, axis=(1, 2)) + jnp.sum(
        bias_rows * bias_rows, axis=1
    )
    clip_square = float(SEQ * D * FF)
    squares = lax.psum(partial_value, "mp") + other_squares * clip_square
    clip_bound = math.sqrt(SEQ * D * FF)
    factor = jnp.minimum(1.0, clip_bound / jnp.sqrt(squares))
    weighted = jnp.sum(factor[:, None, None] * per_grad, axis=0)
    bias_sum = jnp.sum(factor[:, None] * bias_rows, axis=0)
    examples = local_count * lax.axis_size("dp")
    total_weight, total_bias = lax.psum((weighted, bias_sum), "dp")
    share_rows = weight_noise.shape[0]
    total_weight = lax.dynamic_slice_in_dim(
        total_weight, lax.axis_index("dp") * share_rows, share_rows, 0
    )
    weight_grad = (total_weight + weight_noise) / examples
    bias_grad = (total_bias + bias_noise) / examples
    return (input_grad, weight_grad, bias_grad)


def solution(mesh):
    placed = (P("dp", "mp"), P(None, "mp"), P("mp"), P("dp", "mp"), P("dp"), P("dp", "mp"), P("mp"))
    return jax.shard_map(
        per_device,
        mesh=mesh,
        in_specs=placed,
        out_specs=(P("dp", "mp"), P("dp", "mp"), P("mp")),
        check_vma=False,
    )
```

profile of v0, /device:TPU:10, one launch (start us, length us, event | category | flops | bytes accessed | tf_op | source)
XLA Modules:
  0.0 977.1 jit_solution(4633649134920546713)
XLA Ops:
  7.2 0.0 copy-start
  7.2 0.0 all-gather.2.cloned.1.call-start
  7.2 0.7 all-gather.2.cloned.1.call-update
  7.9 0.0 all-reduce.2.cloned.1.call-start
  8.0 47.6 %all-gather.2.cloned.1.call-done = bf16[512,1280]{0,1:T(8,128)(2,1)} async-done(((bf16[512,160]{0,1:T(8,128)(2,1)}), bf16[512,1280]{0,1:T(8,128)(2,1)}) %all-gather.2.cloned.1.call-update) | async-done | bytes 1310736 | tf_op jit(solution)/shard_map/all_gather | solution.py:22
  55.5 0.0 copy-done
  55.5 4.0 convert_reduce_fusion
  59.5 0.1 multiply_reduce_fusion.2
  59.6 1.6 copy.16
  61.2 0.0 copy-start.1
  61.2 0.5 fusion.7
  61.8 0.0 copy-start.5
  61.8 0.5 copy-done.1
  62.3 0.5 fusion.6
  62.8 14.0 %psum.21 = f32[2]{0:T(128)S(1)} all-reduce(f32[2]{0:T(128)S(1)} %add.45), channel_id=1, replica_groups=mesh['dp'=64,'mp'=8] {'mp'}, use_global_device_ids=true, to_apply=%region_4.0 | all-reduce | flops 2 | bytes 16 | tf_op jit(solution)/shard_map/psum | solution.py:48
  76.8 0.0 copy-done.5
  76.8 4.1 multiply_reduce_fusion
  81.0 0.0 copy-start.2
  81.0 0.0 all-reduce.2.cloned.1.call-update
  81.0 0.0 reduce-scatter.2.cloned.1.call-start
  81.0 1.0 copy-done.2
  82.0 2.3 convolution_convert_fusion
  84.3 0.0 copy-start.3
  84.3 0.0 copy-start.4
  84.3 0.0 reduce-scatter.2.cloned.1.call-update
  84.4 0.8 copy-done.3
  85.1 0.2 copy.18
  85.3 0.1 multiply_reduce_fusion.1
  85.4 201.4 %psum.23 = f32[640]{0:T(1024)S(1)} all-reduce(f32[640]{0:T(1024)S(1)} %multiply_reduce_fusion.1), channel_id=1, replica_groups=mesh['dp'=64,'mp'=8] {'dp'}, use_global_device_ids=true, to_apply=%region_8.0 | all-reduce | flops 640 | bytes 5120 | tf_op jit(solution)/shard_map/psum | solution.py:54
  286.8 0.0 copy-done.4
  286.8 0.6 add_multiply_fusion.1
  287.4 628.9 %all-reduce.2.cloned.1.call-done = f32[1280,640]{0,1:T(8,128)} async-done(((f32[1280,640]{0,1:T(8,128)}), f32[1280,640]{0,1:T(8,128)}) %all-reduce.2.cloned.1.call-update) | async-done | bytes 3276816 | tf_op jit(solution)/shard_map/psum | solution.py:54
  916.4 1.2 add_multiply_fusion
  917.6 0.8 copy.19
  918.4 52.2 %reduce-scatter.2.cloned.1.call-done = bf16[512,160]{0,1:T(8,128)(2,1)} async-done(((bf16[512,1280]{0,1:T(8,128)(2,1)}), bf16[512,160]{0,1:T(8,128)(2,1)}) %reduce-scatter.2.cloned.1.call-update) | async-done | bytes 163856 | tf_op jit(solution)/shard_map/reduce_scatter | solution.py:28
  (2 shorter events, 0.0 us)
Async XLA Ops:
  7.2 48.4 %copy-start = (bf16[1280,640]{1,0:T(8,128)(2,1)S(1)}, bf16[1280,640]{1,0:T(8,128)(2,1)}, u32[]{:S(2)}) copy-start(bf16[1280,640]{1,0:T(8,128)(2,1)} %param.8) | copy-start | bytes 4915204
  7.2 48.3 %all-gather.2.cloned.1.call-start = ((), (), s32[]{:S(2)}) async-start(), calls=%async_computation.1 | async-start | bytes 1474560 | tf_op jit(solution)/shard_map/all_gather | solution.py:22
  7.9 908.5 %all-reduce.2.cloned.1.call-start = ((), (), s32[]{:S(2)}) async-start(), calls=%async_computation.3 | async-start | bytes 6553600 | tf_op jit(solution)/shard_map/psum | solution.py:54
  61.2 1.1 copy-start.1
  61.8 15.0 %copy-start.5 = (f32[2]{0:T(128)S(1)}, f32[2]{0:T(128)}, u32[]{:S(2)}) copy-start(f32[2]{0:T(128)} %param.11) | copy-start | bytes 28
  81.0 1.1 copy-start.2
  81.0 889.6 %reduce-scatter.2.cloned.1.call-start = ((), (), s32[]{:S(2)}) async-start(), calls=%async_computation.2 | async-start | bytes 1474560 | tf_op jit(solution)/shard_map/reduce_scatter | solution.py:28
  84.3 0.8 copy-start.3
  84.3 202.5 %copy-start.4 = (f32[640]{0:T(1024)S(1)}, f32[640]{0:T(1024)}, u32[]{:S(2)}) copy-start(f32[640]{0:T(1024)} %param.13) | copy-start | bytes 7684
Sparse Core Ops, SparseCore 0:
  10.1 45.3 all-gather.1
  81.1 835.2 all-reduce.1
  920.0 50.5 reduce-scatter.1
where the time goes:
time: 978 us; the launch traced here: 977 us
  waiting for transfers between devices  729 us (75%)
  blocking collectives  215 us (22%)
  between operations  13.8 us (1%)
  matrix products  11.4 us (1%)
    psum x1, waiting for transfers between devices, per_device(): total_weight, total_bias = lax.psum((weighted, bias_sum), 'dp')  629 us
    psum x1, blocking collectives, per_device(): total_weight, total_bias = lax.psum((weighted, bias_sum), 'dp')  201 us
    reduce_scatter x1, waiting for transfers between devices, per_device(): lax.psum_scatter(back_terms.astype(jnp.bfloat16), 'mp', scatter_dimension...  52.2 us
    all_gather x1, waiting for transfers between devices, per_device(): gathered = lax.all_gather(layer_input, 'mp', axis=1, tiled=True)  47.6 us
  transfers between devices with their start and end apart: 3, of which 3 were waited for; matrix products, arithmetic and copies ran while one was open for 1% of the time, Pallas kernels for 0%

commit v1 on v0

v1 whole, which is shorter than its diff:
```python
import math

import jax
import jax.numpy as jnp
from jax import lax
from jax.experimental import pallas as pl
from jax.experimental.pallas import tpu as pltpu
from jax.sharding import PartitionSpec as P

D = 1280
FF = 5120
SEQ = 256
EXAMPLES = 128
NX, NY, NH = 4, 8, 2
NZ, NC = 4, 2
N_MP = NZ * NC
R = D // N_MP
F = FF // N_MP
CA = 384
CB = F - CA
XR = D // NX
YR = XR // NY
CLIP_SQUARE = float(SEQ * D * FF)
CLIP_BOUND = math.sqrt(SEQ * D * FF)
F32 = jnp.float32
BF16 = jnp.bfloat16


def gelu_slope(pre_act):
    normal_cdf = 0.5 * (1.0 + lax.erf(pre_act * 0.7071067811865476))
    normal_pdf = jnp.exp(-0.5 * pre_act * pre_act) * 0.3989422804014327
    return normal_cdf + pre_act * normal_pdf


def rows(start, size, align=16):
    return pl.ds(pl.multiple_of(start, align), size)


def kernel(
    x_hbm, w_hbm, h_hbm, bias_ref, other_ref,
    ig_ref, wg_ref, bg_ref,
    x_in, w, h, xg, acc, g, per, nt, bt,
    bsend, brecv, bown, zsend, zrecv, igacc,
    wa, ra1, ra2, suma, ya, yra,
    wb, rb, sumb, xb, xrb,
    zs, zsnd, zrcv, bx, by, bz,
    lsem, ag_s, ag_f, ag_p, ag_r, nsem, nrem, ss_s, ss_r, zz_s, zz_r,
    a1_s, a1_r, a2_s, a2_r, ya_s, ya_r, b_s, b_r, xb_s, xb_r, h_s, h_r,
    bx_s, bx_r, by_s, by_r, bz_s, bz_r,
):
    d, m = lax.axis_index("dp"), lax.axis_index("mp")
    px, py, ph = d // (NY * NH), (d // NH) % NY, d % NH
    z, c = m // NC, m % NC
    sibling = (d, m + 1 - 2 * c)

    def at_z(other):
        return (d, other * NC + c)

    def at_x(k):
        return (((px + k) % NX * NY + py) * NH + ph, m)

    def at_y(k):
        return ((px * NY + (py + k) % NY) * NH + ph, m)

    half_peer = (d + 1 - 2 * ph, m)

    def send(src, dst, ssem, rsem, device):
        return pltpu.make_async_remote_copy(
            src_ref=src, dst_ref=dst, send_sem=ssem, recv_sem=rsem,
            device_id=device, device_id_type=pl.DeviceIdType.MESH,
        )

    load_x = pltpu.make_async_copy(x_hbm, x_in, lsem.at[0])
    load_w = pltpu.make_async_copy(w_hbm, w, lsem.at[1])
    load_h = pltpu.make_async_copy(h_hbm, h, lsem.at[2])
    load_x.start()
    load_w.start()
    load_h.start()
    barrier = pltpu.get_barrier_semaphore()

    def greet(device):
        pl.semaphore_signal(barrier, inc=1, device_id=device, device_id_type=pl.DeviceIdType.MESH)

    for k in range(1, N_MP):
        greet((d, (m + k) % N_MP))
    for k in range(1, NX):
        greet(at_x(k))
    for k in range(1, NY):
        greet(at_y(k))
    greet(half_peer)

    load_x.wait()
    for e in range(2):
        xg[e, rows(m * R, R, 32), :] = jnp.transpose(
            x_in[e * SEQ : (e + 1) * SEQ, :].astype(F32)
        ).astype(BF16)
    pl.semaphore_wait(barrier, N_MP - 1 + NX - 1 + NY - 1 + 1)

    def slot(e, i):
        return xg.at[e, rows(i * R, R, 32), :]

    def ag_copy(e, i, ssem, device):
        return send(slot(e, i), slot(e, i), ssem, ag_r.at[e * N_MP + i], device)

    first = jnp.where(z == NZ - 1, 3, 1)
    order = (2, first, 4 - first)

    def far(k):
        other = (z + k) % NZ
        return (other - z == 3) | (z - other == 3)

    def ag_start(e):
        for j, k in enumerate(order):
            @pl.when(jnp.logical_not(far(k)))
            def _(j=j, k=k):
                ag_copy(e, m, ag_s.at[e * 4 + j], at_z((z + k) % NZ)).start()
        ag_copy(e, m, ag_s.at[e * 4 + 3], sibling).start()

    inner = (z == 1) | (z == 2)
    relay_to = at_z(jnp.where(z == 2, 3, 0))

    def ag_take(e, j):
        i = (z + order[j]) % NZ * NC + c
        ag_copy(e, i, ag_s.at[0], sibling).wait_recv()
        if j == 0:
            @pl.when(inner)
            def _():
                ag_copy(e, i, ag_p.at[e], relay_to).start()
        ag_copy(e, i, ag_f.at[e * 3 + j], sibling).start()

    def ag_rest(e):
        for k in range(NZ):
            i = (z + k) % NZ * NC + 1 - c
            ag_copy(e, i, ag_s.at[0], sibling).wait_recv()

    def ag_sent(e):
        for j, k in enumerate(order):
            @pl.when(jnp.logical_not(far(k)))
            def _(j=j, k=k):
                ag_copy(e, m, ag_s.at[e * 4 + j], at_z((z + k) % NZ)).wait_send()
        ag_copy(e, m, ag_s.at[e * 4 + 3], sibling).wait_send()
        for j in range(3):
            ag_copy(e, m, ag_f.at[e * 3 + j], sibling).wait_send()

        @pl.when(inner)
        def _():
            ag_copy(e, m, ag_p.at[e], relay_to).wait_send()

    def pre_act(e):
        acc[...] = jnp.broadcast_to(bias_ref[...], (SEQ, F))

        def step(b, carry):
            at = rows(b * 256, 256, 256)
            acc[...] += lax.dot_general(
                xg[e, at, :], w[at, :], (((0,), (0,)), ((), ())), preferred_element_type=F32
            )
            return carry

        lax.fori_loop(0, D // 256, step, 0)

    def slope(e):
        def step(b, total):
            at = rows(b * 32, 32, 32)
            grad = h[rows(e * SEQ + b * 32, 32, 32), :].astype(F32)
            value = (grad * gelu_slope(acc[at, :])).astype(BF16)
            g[e, at, :] = value
            wide = value.astype(F32)
            return total + wide[0:8] + wide[8:16] + wide[16:24] + wide[24:32]

        total = lax.fori_loop(0, SEQ // 32, step, jnp.zeros((8, F), F32))
        row = jnp.sum(total, axis=0, keepdims=True)
        bt[e] = jnp.zeros((8, 128), F32)
        for k in range(F // 128):
            bt[e, k : k + 1, :] = row[:, k * 128 : (k + 1) * 128]

    def weight_terms(e):
        def step(b, total):
            at = rows(b * 256, 256, 256)
            value = jnp.dot(xg[e, at, :], g[e], preferred_element_type=F32)
            per[e, at, :] = value
            return total + jnp.sum((value * value).reshape(32, 8, F), axis=0)

        total = lax.fori_loop(0, D // 256, step, jnp.zeros((8, F), F32))
        tile = bt[e] * bt[e]
        for k in range(F // 128):
            tile = tile + total[:, k * 128 : (k + 1) * 128]
        nt[e, m] = tile

    def norm_copy(e, i, k):
        return send(
            nt.at[e, i], nt.at[e, i], nsem.at[e * N_MP + k], nrem.at[e * N_MP + i],
            (d, (m + k) % N_MP),
        )

    def norm_start(e):
        for k in range(1, N_MP):
            norm_copy(e, m, k).start()

    def norm_wait(e):
        for k in range(1, N_MP):
            norm_copy(e, (m + k) % N_MP, k).wait_recv()

    def back_half(e, core, store):
        def step(k, carry):
            at = rows((k * NC + core) * R, R, 32)
            store(k, lax.dot_general(
                w[at, :], g[e], (((1,), (1,)), ((), ())), preferred_element_type=F32
            ))
            return carry

        lax.fori_loop(0, NZ, step, 0)

    def pair_copy(e):
        return send(bsend.at[e], brecv.at[e], ss_s.at[e], ss_r.at[e], sibling)

    def back(e):
        def store_other(k, value):
            bsend[e, k] = value.astype(BF16)

        def store_own(k, value):
            bown[e, k] = value

        back_half(e, 1 - c, store_other)
        pair_copy(e).start()
        back_half(e, c, store_own)

    def z_copy(e, k):
        other = (z + k) % NZ
        return send(
            zsend.at[e, other], zrecv.at[e, k - 1], zz_s.at[e * 3 + k - 1], zz_r.at[e * 3 + k - 1],
            at_z(other),
        )

    def back_send(e):
        pair_copy(e).wait_recv()
        for k in (2, 1, 3):
            other = (z + k) % NZ
            zsend[e, other] = (bown[e, other] + brecv[e, other].astype(F32)).astype(BF16)
            z_copy(e, k).start()
        igacc[e] = bown[e, z] + brecv[e, z].astype(F32)

    def back_take(e):
        total = igacc[e]
        for k in range(1, NZ):
            z_copy(e, k).wait_recv()
            total = total + zrecv[e, k - 1].astype(F32)
        ig_ref[:, e * SEQ : (e + 1) * SEQ] = total.astype(BF16)

    ag_start(0)
    load_w.wait()
    load_h.wait()
    ag_start(1)
    for j in range(3):
        ag_take(0, j)
    ag_rest(0)
    pre_act(0)
    slope(0)
    ag_take(1, 0)
    weight_terms(0)
    norm_start(0)
    ag_take(1, 1)
    back(0)
    ag_take(1, 2)
    ag_rest(1)
    pre_act(1)
    slope(1)
    weight_terms(1)
    norm_start(1)
    back_send(0)
    back(1)
    norm_wait(0)
    norm_wait(1)

    factors = []
    for e in range(2):
        tile = nt[e, 0]
        for i in range(1, N_MP):
            tile = tile + nt[e, i]
        squares = jnp.full((1, 128), jnp.sum(tile) + other_ref[e] * CLIP_SQUARE, F32)
        factors.append(jnp.minimum(1.0, CLIP_BOUND / jnp.sqrt(squares)))
    f0, f1 = factors
    f0a, f1a = jnp.tile(f0, (1, CA // 128)), jnp.tile(f1, (1, CA // 128))
    f0b, f1b = jnp.tile(f0, (1, CB // 128)), jnp.tile(f1, (1, CB // 128))

    def weighted_a(at):
        return f0a * per[0, at, 0:CA] + f1a * per[1, at, 0:CA]

    def weighted_b(at):
        return f0b * per[0, at, CA:F] + f1b * per[1, at, CA:F]

    def fill_a(k):
        owner = (px + k) % NX
        for half in range(2):
            wa[owner * 2 + half] = weighted_a(rows(owner * XR + half * R, R, 32)).astype(BF16)

    def block_b(owner):
        return jnp.concatenate(
            [weighted_b(rows(i * XR + owner * YR, YR, 8)) for i in range(NX)], axis=0
        )

    def fill_b(k):
        owner = (py + k) % NY
        wb[owner] = block_b(owner).astype(BF16)

    right, left = 1, NX - 1

    def a1_copy(way):
        return send(
            wa.at[(px + 2) % NX * 2 + way], ra1.at[way], a1_s.at[way], a1_r.at[way],
            at_x((right, left)[way]),
        )

    def a2_copy(way, half):
        k = (right, left)[way]
        return send(
            wa.at[(px + k) % NX * 2 + half], ra2.at[way, half], a2_s.at[way * 2 + half],
            a2_r.at[way * 2 + half], at_x(k),
        )

    def b_copy(way, k):
        owner = (py + (k if way == 0 else NY - k)) % NY
        part = (slice(0, 80) if way == 0 else slice(80, 160)) if k == 4 else slice(0, 160)
        return send(
            wb.at[owner, part], rb.at[way, k - 1, part], b_s.at[way * 4 + k - 1],
            b_r.at[way * 4 + k - 1], at_y(1 if way == 0 else NY - 1),
        )

    def b_step(k):
        for way in range(2):
            owner = (py + (k if way == 0 else NY - k)) % NY
            b_copy(way, k + 1).wait_recv()
            part = (slice(0, 80) if way == 0 else slice(80, 160)) if k == 3 else slice(0, 160)
            wb[owner, part] = (
                wb[owner, part].astype(F32) + rb[way, k, part].astype(F32)
            ).astype(BF16)
            b_copy(way, k).start()

    def bx_copy(i, k):
        return send(bx.at[i], bx.at[i], bx_s.at[k], bx_r.at[i], at_x(k))

    def by_copy(i, k):
        return send(by.at[i], by.at[i], by_s.at[k], by_r.at[i], at_y(k))

    def bz_copy(i):
        return send(bz.at[i], bz.at[i], bz_s.at[0], bz_r.at[i], half_peer)

    fill_a(2)
    a1_copy(0).start()
    a1_copy(1).start()
    fill_b(4)
    b_copy(0, 4).start()
    b_copy(1, 4).start()
    bx[px] = f0 * bt[0] + f1 * bt[1]
    for k in range(1, NX):
        bx_copy(px, k).start()
    fill_a(1)
    a2_copy(0, 1).start()
    fill_a(3)
    a2_copy(1, 0).start()
    for k in (3, 5, 2, 6, 1, 7):
        fill_b(k)
    b_step(3)
    back_send(1)
    for way in range(2):
        a1_copy(way).wait_recv()
        at = (px + (right, left)[way]) % NX * 2 + way
        wa[at] = (wa[at].astype(F32) + ra1[way].astype(F32)).astype(BF16)
        a2_copy(way, way).start()
    b_step(2)
    for k in range(1, NX):
        bx_copy((px + k) % NX, k).wait_recv()
    by[py] = (bx[0] + bx[1]) + (bx[2] + bx[3])
    for k in range(1, NY):
        by_copy(py, k).start()

    for way in range(2):
        for half in range(2):
            a2_copy(way, half).wait_recv()
    for half in range(2):
        suma[half * R : (half + 1) * R, :] = (
            weighted_a(rows(px * XR + half * R, R, 32))
            + ra2[0, half].astype(F32)
            + ra2[1, half].astype(F32)
        )

    def pack_a(owner):
        block = suma[rows(owner * YR, YR, 8), :]
        parts = [block[:, k * 128 : (k + 1) * 128] for k in range(CA // 128)]
        return jnp.concatenate(parts + [jnp.zeros((8, 128), F32)], axis=0)

    def ya_copy(k):
        return send(
            ya.at[k - 1], yra.at[k - 1], ya_s.at[k - 1], ya_r.at[k - 1], at_y(k)
        )

    for k in (4, 3, 5, 2, 6, 1, 7):
        ya[k - 1] = pack_a((py + k) % NY).astype(BF16)
        ya_copy(k).start()
    b_step(1)
    for way in range(2):
        b_copy(way, 1).wait_recv()
    sumb[...] = block_b(py) + rb[0, 0].astype(F32) + rb[1, 0].astype(F32)

    def pack_b(owner):
        block = sumb[rows(owner * YR, YR, 8), :]
        return jnp.concatenate([block[:, 0:128], block[:, 128:256]], axis=0)

    def xb_copy(k):
        return send(xb.at[k - 1], xrb.at[k - 1], xb_s.at[k - 1], xb_r.at[k - 1], at_x(k))

    for k in (2, 1, 3):
        xb[k - 1] = pack_b((px + k) % NX).astype(BF16)
        xb_copy(k).start()

    for k in range(1, NY):
        by_copy((py + k) % NY, k).wait_recv()
    total = by[0]
    for i in range(1, NY):
        total = total + by[i]
    bz[ph] = total
    bz_copy(ph).start()

    back_take(0)
    back_take(1)

    total = pack_a(py)
    for k in range(1, NY):
        ya_copy(k).wait_recv()
        total = total + yra[k - 1].astype(F32)
    zs[0:120, :] = total[0:120]
    total = pack_b(px)
    for k in range(1, NX):
        xb_copy(k).wait_recv()
        total = total + xrb[k - 1].astype(F32)
    zs[120:200, :] = total

    def of_half(half):
        return [zs[rows(i * YR + half * 16, 24, 8), :] for i in range(F // 128)]

    zsnd[...] = jnp.concatenate(of_half(1 - ph) + [jnp.zeros((8, 128), F32)], axis=0).astype(BF16)
    half_copy = send(zsnd, zrcv, h_s.at[0], h_r.at[0], half_peer)
    half_copy.start()
    bz_copy(1 - ph).wait_recv()
    bg_ref[...] = bz[0] + bz[1]
    mine = of_half(ph)
    half_copy.wait_recv()
    theirs = zrcv[...].astype(F32)
    for i in range(F // 128):
        wg_ref[:, i * 128 : (i + 1) * 128] = mine[i] + theirs[i * 24 : (i + 1) * 24]

    for e in range(2):
        ag_sent(e)
        for k in range(1, N_MP):
            norm_copy(e, m, k).wait_send()
        pair_copy(e).wait_send()
        for k in range(1, NZ):
            z_copy(e, k).wait_send()
    for way in range(2):
        a1_copy(way).wait_send()
        for half in range(2):
            a2_copy(way, half).wait_send()
        for k in range(1, 5):
            b_copy(way, k).wait_send()
    for k in range(1, NY):
        ya_copy(k).wait_send()
        by_copy(py, k).wait_send()
    for k in range(1, NX):
        xb_copy(k).wait_send()
        bx_copy(px, k).wait_send()
    bz_copy(ph).wait_send()
    half_copy.wait_send()


def fused(layer_input, first_weight, hidden_grad, first_bias, other_squares):
    vmem = pl.BlockSpec(memory_space=pltpu.VMEM)
    anywhere = pl.BlockSpec(memory_space=pl.ANY)
    dma = pltpu.SemaphoreType.DMA

    def buf(shape, dtype=BF16):
        return pltpu.VMEM(shape, dtype)

    return pl.pallas_call(
        kernel,
        out_shape=(
            jax.ShapeDtypeStruct((R, 2 * SEQ), BF16),
            jax.ShapeDtypeStruct((24, F), F32),
            jax.ShapeDtypeStruct((8, 128), F32),
        ),
        in_specs=[anywhere] * 3 + [vmem, pl.BlockSpec(memory_space=pltpu.SMEM)],
        out_specs=(vmem, vmem, vmem),
        scratch_shapes=[
            buf((2 * SEQ, R)), buf((D, F)), buf((2 * SEQ, F)),
            buf((2, D, SEQ)), buf((SEQ, F), F32), buf((2, SEQ, F)),
            buf((2, D, F), F32), buf((2, N_MP, 8, 128), F32), buf((2, 8, 128), F32),
            buf((2, NZ, R, SEQ)), buf((2, NZ, R, SEQ)), buf((2, NZ, R, SEQ), F32),
            buf((2, NZ, R, SEQ)), buf((2, NZ - 1, R, SEQ)), buf((2, R, SEQ), F32),
            buf((8, R, CA)), buf((2, R, CA)), buf((2, 2, R, CA)),
            buf((XR, CA), F32), buf((NY - 1, 128, 128)), buf((NY - 1, 128, 128)),
            buf((NY, 160, CB)), buf((2, 4, 160, CB)), buf((160, CB), F32),
            buf((NX - 1, 80, 128)), buf((NX - 1, 80, 128)),
            buf((200, 128), F32), buf((128, 128)), buf((128, 128)),
            buf((NX, 8, 128), F32), buf((NY, 8, 128), F32), buf((NH, 8, 128), F32),
            dma((3,)), dma((8,)), dma((6,)), dma((2,)), dma((16,)),
            dma((16,)), dma((16,)), dma((2,)), dma((2,)), dma((6,)), dma((6,)),
            dma((2,)), dma((2,)), dma((4,)), dma((4,)), dma((7,)), dma((7,)),
            dma((8,)), dma((8,)), dma((3,)), dma((3,)), dma((1,)), dma((1,)),
            dma((NX,)), dma((NX,)), dma((NY,)), dma((NY,)), dma((1,)), dma((NH,)),
        ],
        compiler_params=pltpu.CompilerParams(
            collective_id=0, has_side_effects=True, vmem_limit_bytes=40 * 2**20
        ),
        cost_estimate=pl.CostEstimate(
            flops=6 * 512 * D * F, bytes_accessed=3 * 2**20, transcendentals=2 * 512 * F
        ),
    )(layer_input, first_weight, hidden_grad, first_bias.reshape(1, F), other_squares)


def per_device(
    layer_input, first_weight, first_bias, hidden_grad, other_squares, weight_noise, bias_noise
):
    input_t, weight_sum, bias_sum = fused(
        layer_input, first_weight, hidden_grad, first_bias, other_squares
    )
    half = lax.axis_index("dp") % NH
    mine = lax.dynamic_slice_in_dim(weight_sum, half * 4, weight_noise.shape[0], 0)
    weight_grad = (mine + weight_noise) / EXAMPLES
    bias_grad = (bias_sum[: F // 128].reshape(F) + bias_noise) / EXAMPLES
    return (input_t.T, weight_grad, bias_grad)


def solution(mesh):
    placed = (P("dp", "mp"), P(None, "mp"), P("mp"), P("dp", "mp"), P("dp"), P("dp", "mp"), P("mp"))
    return jax.shard_map(
        per_device,
        mesh=mesh,
        in_specs=placed,
        out_specs=(P("dp", "mp"), P("dp", "mp"), P("mp")),
        check_vma=False,
    )
```

time: 978 us -> 78 us (0.08)
  the two profiles are of different devices: /device:TPU:10 before, /device:TPU:2 now
where the time goes in v1:
time: 78 us; the launch traced here: 77.7 us
  Pallas kernels  70.2 us (90%)
  local copies, waits for them, and re-layouts  5.58 us (7%)
  other arithmetic  1.24 us (2%)
    pallas_call x1, Pallas kernels, fused(): pl.pallas_call(kernel, out_shape=(jax.ShapeDtypeStruct((R, 2 * SEQ), BF16...  70.2 us
    unnamed x12, local copies, waits for them, and re-layouts  4.89 us

profile of v1, /device:TPU:2, one launch (start us, length us, event | category | flops | bytes accessed | tf_op | source)
XLA Modules:
  0.0 77.7 jit_solution(1906493437753608028)
XLA Ops:
  0.6 1.0 %copy.10.x_hbm = bf16[512,160]{1,0:T(8,128)(2,1)S(1)} copy(bf16[512,160]{0,1:T(8,128)(2,1)} %param.7) | data formatting | bytes 327680 | tf_op args[0]
  1.7 0.7 reshape.12.bias_ref
  2.4 0.0 copy-start
  2.4 1.4 %copy-done = bf16[1280,640]{1,0:T(8,128)(2,1)S(1)} copy-done((bf16[1280,640]{1,0:T(8,128)(2,1)S(1)}, bf16[1280,640]{1,0:T(8,128)(2,1)}, u32[]{:S(2)}) %copy-start) | copy-done | bytes 1638424
  3.8 0.0 copy-start.1
  3.8 1.1 %copy-done.1 = bf16[512,640]{1,0:T(8,128)(2,1)S(1)} copy-done((bf16[512,640]{1,0:T(8,128)(2,1)S(1)}, bf16[512,640]{1,0:T(8,128)(2,1)}, u32[]{:S(2)}) %copy-start.1) | copy-done | bytes 655384
  4.9 0.0 copy-start.2
  4.9 0.7 copy-done.2
  5.6 0.0 copy-start.3
  5.6 0.0 copy-start.4
  5.6 70.2 %shard_map.94 = (bf16[160,512]{1,0:T(8,128)(2,1)S(1)}, f32[24,640]{1,0:T(8,128)S(1)}, f32[8,128]{1,0:T(8,128)S(1)}) custom-call(bf16[512,160]{1,0:T(8,128)(2,1)S(1)} %copy.10.x_hbm, bf16[1280,640]{1,0:T(8,128)(2,1)S(1)} %copy-done, bf16[512,640]{1,0:T(8,128)(2,1)S(1)} %copy-done.1, f32[1,640]{1,0:T(1,128)S(1)} %reshape.12.bias_ref, f32[2]{0:T(128)S(1)} %copy-done.2), custom_call_target="tpu_custom_call" | custom-call | flops 2516582400 | bytes 3145728 | tf_op jit(solution)/shard_map/pallas_call | solution.py:482
  75.8 0.0 copy-done.3
  75.8 0.6 add_multiply_fusion
  76.5 0.0 copy-done.4
  76.5 0.6 fusion
  77.1 0.7 copy.12
Async XLA Ops:
  2.4 1.4 %copy-start = (bf16[1280,640]{1,0:T(8,128)(2,1)S(1)}, bf16[1280,640]{1,0:T(8,128)(2,1)}, u32[]{:S(2)}) copy-start(bf16[1280,640]{1,0:T(8,128)(2,1)} %w_hbm.1) | copy-start | bytes 4915204
  3.8 1.1 %copy-start.1 = (bf16[512,640]{1,0:T(8,128)(2,1)S(1)}, bf16[512,640]{1,0:T(8,128)(2,1)}, u32[]{:S(2)}) copy-start(bf16[512,640]{1,0:T(8,128)(2,1)} %h_hbm.1) | copy-start | bytes 1966084
  4.9 0.7 copy-start.2
  5.6 70.3 %copy-start.3 = (f32[20,640]{1,0:T(8,128)S(1)}, f32[20,640]{1,0:T(8,128)}, u32[]{:S(2)}) copy-start(f32[20,640]{1,0:T(8,128)} %param.12) | copy-start | bytes 153604
  5.6 70.9 %copy-start.4 = (f32[640]{0:T(1024)S(1)}, f32[640]{0:T(1024)}, u32[]{:S(2)}) copy-start(f32[640]{0:T(1024)} %param.13) | copy-start | bytes 7684

commit v2 on v1

v2 whole, which is shorter than its diff:
```python
import math

import jax
import jax.numpy as jnp
from jax import lax
from jax.experimental import pallas as pl
from jax.experimental.pallas import tpu as pltpu
from jax.sharding import PartitionSpec as P

D = 1280
FF = 5120
SEQ = 256
EXAMPLES = 128
NX, NY, NH = 4, 8, 2
NZ, NC = 4, 2
N_MP = NZ * NC
R = D // N_MP
F = FF // N_MP
NA = 3
NB = F // 128 - NA
XR = D // NX
YR = XR // NY
CLIP_SQUARE = float(SEQ * D * FF)
CLIP_BOUND = math.sqrt(SEQ * D * FF)
F32 = jnp.float32
BF16 = jnp.bfloat16


def gelu_slope(pre_act):
    normal_cdf = 0.5 * (1.0 + lax.erf(pre_act * 0.7071067811865476))
    normal_pdf = jnp.exp(-0.5 * pre_act * pre_act) * 0.3989422804014327
    return normal_cdf + pre_act * normal_pdf


def rows(start, size, align=16):
    return pl.ds(pl.multiple_of(start, align), size)


def kernel(
    x_hbm, w_hbm, h_hbm, bias_hbm, other_hbm,
    ig_ref, wg_ref, bg_ref,
    w, h, bias, other_ref, xg, acc, g, per, nt, bt,
    bsend, brecv, bown, zsend, zrecv, igacc,
    wa, ra1, ra2, suma, ya, yra,
    wb, rb, sumb, xb, xrb,
    zs, zsnd, zrcv, bx, by, bz,
    lsem, ag_s, ag_f, ag_p, ag_r, nsem, nrem, ss_s, ss_r, zz_s, zz_r,
    a1_s, a1_r, a2_s, a2_r, ya_s, ya_r, b_s, b_r, xb_s, xb_r, h_s, h_r,
    bx_s, bx_r, by_s, by_r, bz_s, bz_r,
):
    d, m = lax.axis_index("dp"), lax.axis_index("mp")
    px, py, ph = d // (NY * NH), (d // NH) % NY, d % NH
    z, c = m // NC, m % NC
    sibling = (d, m + 1 - 2 * c)

    def at_z(other):
        return (d, other * NC + c)

    def at_x(k):
        return (((px + k) % NX * NY + py) * NH + ph, m)

    def at_y(k):
        return ((px * NY + (py + k) % NY) * NH + ph, m)

    half_peer = (d + 1 - 2 * ph, m)

    def send(src, dst, ssem, rsem, device):
        return pltpu.make_async_remote_copy(
            src_ref=src, dst_ref=dst, send_sem=ssem, recv_sem=rsem,
            device_id=device, device_id_type=pl.DeviceIdType.MESH,
        )

    pending = []

    def start(copy, when=None):
        if when is None:
            copy.start()
        else:
            pl.when(when)(copy.start)
        pending.append((copy, when))

    load_x = [
        pltpu.make_async_copy(
            x_hbm.at[:, e * SEQ : (e + 1) * SEQ], xg.at[e, rows(m * R, R, 32), :], lsem.at[e]
        )
        for e in range(2)
    ]
    loads = [
        pltpu.make_async_copy(source, target, lsem.at[2 + i])
        for i, (source, target) in enumerate(
            ((w_hbm, w), (h_hbm, h), (bias_hbm, bias), (other_hbm, other_ref))
        )
    ]
    for load in load_x + loads:
        load.start()
    barrier = pltpu.get_barrier_semaphore()

    def greet(device):
        pl.semaphore_signal(barrier, inc=1, device_id=device, device_id_type=pl.DeviceIdType.MESH)

    for k in range(1, N_MP):
        greet((d, (m + k) % N_MP))
    for k in range(1, NX):
        greet(at_x(k))
    for k in range(1, NY):
        greet(at_y(k))
    greet(half_peer)

    load_x[0].wait()
    load_x[1].wait()
    pl.semaphore_wait(barrier, N_MP - 1 + NX - 1 + NY - 1 + 1)

    def slot(e, i):
        return xg.at[e, rows(i * R, R, 32), :]

    def ag_copy(e, i, ssem, device):
        return send(slot(e, i), slot(e, i), ssem, ag_r.at[e * N_MP + i], device)

    first = jnp.where(z == NZ - 1, 3, 1)
    order = (2, first, 4 - first)

    def far(k):
        other = (z + k) % NZ
        return (other - z == 3) | (z - other == 3)

    def ag_start(e):
        for j, k in enumerate(order):
            start(ag_copy(e, m, ag_s.at[e * 4 + j], at_z((z + k) % NZ)), jnp.logical_not(far(k)))
        start(ag_copy(e, m, ag_s.at[e * 4 + 3], sibling))

    inner = (z == 1) | (z == 2)
    relay_to = at_z(jnp.where(z == 2, 3, 0))

    def ag_take(e, j):
        i = (z + order[j]) % NZ * NC + c
        ag_copy(e, i, ag_s.at[0], sibling).wait_recv()
        if j == 0:
            start(ag_copy(e, i, ag_p.at[e], relay_to), inner)
        start(ag_copy(e, i, ag_f.at[e * 3 + j], sibling))

    def ag_rest(e):
        for k in range(NZ):
            i = (z + k) % NZ * NC + 1 - c
            ag_copy(e, i, ag_s.at[0], sibling).wait_recv()

    def pre_act(e):
        acc[...] = lax.dot_general(
            xg[e], w[...], (((0,), (0,)), ((), ())), preferred_element_type=F32
        ) + bias[...].reshape(1, F)

    def slope(e):
        def step(b, total):
            at = rows(b * 32, 32, 32)
            grad = h[rows(e * SEQ + b * 32, 32, 32), :].astype(F32)
            value = (grad * gelu_slope(acc[at, :])).astype(BF16)
            g[e, at, :] = value
            wide = value.astype(F32)
            return total + wide[0:8] + wide[8:16] + wide[16:24] + wide[24:32]

        total = lax.fori_loop(0, SEQ // 32, step, jnp.zeros((8, F), F32))
        row = jnp.sum(total, axis=0, keepdims=True)
        bt[e] = jnp.zeros((8, 128), F32)
        for k in range(F // 128):
            bt[e, k : k + 1, :] = row[:, k * 128 : (k + 1) * 128]

    def weight_terms(e):
        total = jnp.zeros((8, F), F32)
        for b in range(D // 256):
            at = slice(b * 256, (b + 1) * 256)
            value = jnp.dot(xg[e, at, :], g[e], preferred_element_type=F32)
            per[e, at, :] = value
            total = total + jnp.sum((value * value).reshape(32, 8, F), axis=0)
        tile = bt[e] * bt[e]
        for k in range(F // 128):
            tile = tile + total[:, k * 128 : (k + 1) * 128]
        nt[e, m] = tile

    def norm_copy(e, i, k):
        return send(
            nt.at[e, i], nt.at[e, i], nsem.at[e * N_MP + k], nrem.at[e * N_MP + i],
            (d, (m + k) % N_MP),
        )

    def norm_start(e):
        for k in range(1, N_MP):
            start(norm_copy(e, m, k))

    def norm_wait(e):
        for k in range(1, N_MP):
            norm_copy(e, (m + k) % N_MP, k).wait_recv()

    def back_half(e, core, store):
        for k in range(NZ):
            at = rows((k * NC + core) * R, R, 32)
            store(k, lax.dot_general(
                w[at, :], g[e], (((1,), (1,)), ((), ())), preferred_element_type=F32
            ))

    def pair_copy(e):
        return send(bsend.at[e], brecv.at[e], ss_s.at[e], ss_r.at[e], sibling)

    def back(e):
        def store_other(k, value):
            bsend[e, k] = value.astype(BF16)

        def store_own(k, value):
            bown[e, k] = value

        back_half(e, 1 - c, store_other)
        start(pair_copy(e))
        back_half(e, c, store_own)

    def z_copy(e, k):
        other = (z + k) % NZ
        return send(
            zsend.at[e, other], zrecv.at[e, k - 1], zz_s.at[e * 3 + k - 1], zz_r.at[e * 3 + k - 1],
            at_z(other),
        )

    def back_send(e):
        pair_copy(e).wait_recv()
        for k in (2, 1, 3):
            other = (z + k) % NZ
            zsend[e, other] = (bown[e, other] + brecv[e, other].astype(F32)).astype(BF16)
            start(z_copy(e, k))
        igacc[e] = bown[e, z] + brecv[e, z].astype(F32)

    def back_take(e):
        total = igacc[e]
        for k in range(1, NZ):
            z_copy(e, k).wait_recv()
            total = total + zrecv[e, k - 1].astype(F32)
        ig_ref[:, e * SEQ : (e + 1) * SEQ] = total.astype(BF16)

    ag_start(0)
    ag_start(1)
    for load in loads:
        load.wait()
    for j in range(3):
        ag_take(0, j)
    ag_rest(0)
    pre_act(0)
    slope(0)
    ag_take(1, 0)
    weight_terms(0)
    norm_start(0)
    ag_take(1, 1)
    back(0)
    ag_take(1, 2)
    ag_rest(1)
    pre_act(1)
    slope(1)
    weight_terms(1)
    norm_start(1)
    back_send(0)
    back(1)
    norm_wait(0)
    norm_wait(1)

    factors = []
    for e in range(2):
        tile = nt[e, 0]
        for i in range(1, N_MP):
            tile = tile + nt[e, i]
        squares = jnp.full((1, 128), jnp.sum(tile) + other_ref[e] * CLIP_SQUARE, F32)
        factors.append(jnp.minimum(1.0, CLIP_BOUND / jnp.sqrt(squares)))
    f0, f1 = factors

    def weighted(tile, start, size, align=32):
        at, columns = rows(start, size, align), slice(tile * 128, (tile + 1) * 128)
        return f0 * per[0, at, columns] + f1 * per[1, at, columns]

    def weighted_a(t, i):
        return weighted(t, i * R, R)

    def weighted_b(t, owner):
        return jnp.concatenate(
            [weighted(NA + t, i * XR + owner * YR, YR, 8) for i in range(NX)], axis=0
        )

    step_x = (1, NX - 1)
    step_y = (1, NY - 1)

    def index_a(k, half):
        return (px + k) % NX * 2 + half

    def index_b(way, k):
        return (py + (k if way == 0 else NY - k)) % NY

    def a1_copy(t, way):
        return send(
            wa.at[t, index_a(2, way)], ra1.at[t, way], a1_s.at[t * 2 + way], a1_r.at[t * 2 + way],
            at_x(step_x[way]),
        )

    def a2_copy(t, way, half):
        n = (t * 2 + way) * 2 + half
        return send(
            wa.at[t, index_a(step_x[way], half)], ra2.at[t, way, half], a2_s.at[n], a2_r.at[n],
            at_x(step_x[way]),
        )

    def part_b(way, k):
        return (slice(0, 80), slice(80, 160))[way] if k == 4 else slice(0, 160)

    def b_copy(t, way, k):
        n, part = (t * 2 + way) * 4 + k - 1, part_b(way, k)
        return send(
            wb.at[t, index_b(way, k), part], rb.at[t, way, k - 1, part], b_s.at[n], b_r.at[n],
            at_y(step_y[way]),
        )

    def b_step(t, k):
        for way in range(2):
            owner = index_b(way, k)
            b_copy(t, way, k + 1).wait_recv()
            part = part_b(way, k + 1)
            wb[t, owner, part] = (
                wb[t, owner, part].astype(F32) + rb[t, way, k, part].astype(F32)
            ).astype(BF16)
            start(b_copy(t, way, k))

    def bx_copy(i, k):
        return send(bx.at[i], bx.at[i], bx_s.at[k], bx_r.at[i], at_x(k))

    def by_copy(i, k):
        return send(by.at[i], by.at[i], by_s.at[k], by_r.at[i], at_y(k))

    def bz_copy(i):
        return send(bz.at[i], bz.at[i], bz_s.at[0], bz_r.at[i], half_peer)

    def a2_own(t):
        for way in range(2):
            i = index_a(step_x[way], 1 - way)
            wa[t, i] = weighted_a(t, i).astype(BF16)
            start(a2_copy(t, way, 1 - way))

    def a2_sum(t):
        for way in range(2):
            i = index_a(step_x[way], way)
            value = weighted_a(t, i)
            a1_copy(t, way).wait_recv()
            wa[t, i] = (value + ra1[t, way].astype(F32)).astype(BF16)
            start(a2_copy(t, way, way))

    def ya_copy(t, k):
        n = t * (NY - 1) + k - 1
        return send(ya.at[t, k - 1], yra.at[t, k - 1], ya_s.at[n], ya_r.at[n], at_y(k))

    def pad(value, size):
        return jnp.concatenate([value, jnp.zeros((size - value.shape[0], 128), F32)], axis=0)

    def a_turn(t):
        for half in range(2):
            value = weighted_a(t, px * 2 + half)
            for way in range(2):
                a2_copy(t, way, half).wait_recv()
                value = value + ra2[t, way, half].astype(F32)
            suma[t, half * R : (half + 1) * R, :] = value
        for k in (4, 3, 5, 2, 6, 1, 7):
            block = suma[t, rows((py + k) % NY * YR, YR, 8), :]
            ya[t, k - 1] = pad(block, 48).astype(BF16)
            start(ya_copy(t, k))

    def a_take(t):
        total = suma[t, rows(py * YR, YR, 8), :]
        for k in range(1, NY):
            ya_copy(t, k).wait_recv()
            total = total + yra[t, k - 1].astype(F32)[0:YR]
        zs[t * YR : (t + 1) * YR, :] = total

    def xb_copy(k):
        return send(xb.at[k - 1], xrb.at[k - 1], xb_s.at[k - 1], xb_r.at[k - 1], at_x(k))

    def pack_b(owner):
        at = rows(owner * YR, YR, 8)
        return jnp.concatenate([sumb[t, at, :] for t in range(NB)], axis=0)

    for t in range(NA):
        for way in range(2):
            i = index_a(2, way)
            wa[t, i] = weighted_a(t, i).astype(BF16)
            start(a1_copy(t, way))
    for t in range(NB):
        owner = (py + 4) % NY
        wb[t, owner] = weighted_b(t, owner).astype(BF16)
        for way in range(2):
            start(b_copy(t, way, 4))
    a2_own(0)
    bx[px] = f0 * bt[0] + f1 * bt[1]
    for k in range(1, NX):
        start(bx_copy(px, k))
    for k in (3, 5, 2, 6, 1, 7):
        owner = (py + k) % NY
        for t in range(NB):
            wb[t, owner] = weighted_b(t, owner).astype(BF16)
    for t in range(NB):
        b_step(t, 3)
    a2_sum(0)
    a2_own(1)
    a2_sum(1)
    a2_own(2)
    a2_sum(2)
    back_send(1)
    for k in range(1, NX):
        bx_copy((px + k) % NX, k).wait_recv()
    by[py] = (bx[0] + bx[1]) + (bx[2] + bx[3])
    for k in range(1, NY):
        start(by_copy(py, k))
    for t in range(NB):
        b_step(t, 2)
    a_turn(0)
    b_step(0, 1)
    a_turn(1)
    b_step(1, 1)
    a_turn(2)

    for t in range(NB):
        value = weighted_b(t, py)
        for way in range(2):
            b_copy(t, way, 1).wait_recv()
            value = value + rb[t, way, 0].astype(F32)
        sumb[t] = value
    for k in (2, 1, 3):
        xb[k - 1] = pack_b((px + k) % NX).astype(BF16)
        start(xb_copy(k))

    for k in range(1, NY):
        by_copy((py + k) % NY, k).wait_recv()
    total = by[0]
    for i in range(1, NY):
        total = total + by[i]
    bz[ph] = total
    start(bz_copy(ph))

    back_take(0)
    back_take(1)
    a_take(0)
    a_take(1)
    total = pack_b(px)
    for k in range(1, NX):
        xb_copy(k).wait_recv()
        total = total + xrb[k - 1].astype(F32)
    zs[NA * YR :, :] = total
    a_take(2)

    def of_half(half):
        return [zs[rows(i * YR + half * 16, 24, 8), :] for i in range(F // 128)]

    zsnd[...] = pad(jnp.concatenate(of_half(1 - ph), axis=0), 128).astype(BF16)
    half_copy = send(zsnd, zrcv, h_s.at[0], h_r.at[0], half_peer)
    start(half_copy)
    bz_copy(1 - ph).wait_recv()
    bg_ref[...] = bz[0] + bz[1]
    mine = of_half(ph)
    half_copy.wait_recv()
    theirs = zrcv[...].astype(F32)
    for i in range(F // 128):
        wg_ref[:, i * 128 : (i + 1) * 128] = mine[i] + theirs[i * 24 : (i + 1) * 24]

    for copy, when in pending:
        if when is None:
            copy.wait_send()
        else:
            pl.when(when)(copy.wait_send)


def fused(layer_input, first_weight, hidden_grad, first_bias, other_squares):
    vmem = pl.BlockSpec(memory_space=pltpu.VMEM)
    hbm = pl.BlockSpec(memory_space=pltpu.HBM)
    dma = pltpu.SemaphoreType.DMA

    def buf(shape, dtype=BF16):
        return pltpu.VMEM(shape, dtype)

    return pl.pallas_call(
        kernel,
        out_shape=(
            jax.ShapeDtypeStruct((R, 2 * SEQ), BF16),
            jax.ShapeDtypeStruct((24, F), F32),
            jax.ShapeDtypeStruct((8, 128), F32),
        ),
        in_specs=[hbm] * 5,
        out_specs=(vmem, vmem, vmem),
        scratch_shapes=[
            buf((D, F)), buf((2 * SEQ, F)), buf((F,), F32), pltpu.SMEM((2,), F32),
            buf((2, D, SEQ)), buf((SEQ, F), F32), buf((2, SEQ, F)),
            buf((2, D, F), F32), buf((2, N_MP, 8, 128), F32), buf((2, 8, 128), F32),
            buf((2, NZ, R, SEQ)), buf((2, NZ, R, SEQ)), buf((2, NZ, R, SEQ), F32),
            buf((2, NZ, R, SEQ)), buf((2, NZ - 1, R, SEQ)), buf((2, R, SEQ), F32),
            buf((NA, 8, R, 128)), buf((NA, 2, R, 128)), buf((NA, 2, 2, R, 128)),
            buf((NA, XR, 128), F32), buf((NA, NY - 1, 48, 128)), buf((NA, NY - 1, 48, 128)),
            buf((NB, NY, 160, 128)), buf((NB, 2, 4, 160, 128)), buf((NB, 160, 128), F32),
            buf((NX - 1, 80, 128)), buf((NX - 1, 80, 128)),
            buf((200, 128), F32), buf((128, 128)), buf((128, 128)),
            buf((NX, 8, 128), F32), buf((NY, 8, 128), F32), buf((NH, 8, 128), F32),
            dma((6,)), dma((8,)), dma((6,)), dma((2,)), dma((16,)),
            dma((16,)), dma((16,)), dma((2,)), dma((2,)), dma((6,)), dma((6,)),
            dma((NA * 2,)), dma((NA * 2,)), dma((NA * 4,)), dma((NA * 4,)),
            dma((NA * 7,)), dma((NA * 7,)),
            dma((NB * 8,)), dma((NB * 8,)), dma((3,)), dma((3,)), dma((1,)), dma((1,)),
            dma((NX,)), dma((NX,)), dma((NY,)), dma((NY,)), dma((1,)), dma((NH,)),
        ],
        compiler_params=pltpu.CompilerParams(
            collective_id=0, has_side_effects=True, vmem_limit_bytes=60 * 2**20
        ),
        cost_estimate=pl.CostEstimate(
            flops=6 * 512 * D * F, bytes_accessed=3 * 2**20, transcendentals=2 * 512 * F
        ),
    )(layer_input.T, first_weight, hidden_grad, first_bias, other_squares)


def per_device(
    layer_input, first_weight, first_bias, hidden_grad, other_squares, weight_noise, bias_noise
):
    input_t, weight_sum, bias_sum = fused(
        layer_input, first_weight, hidden_grad, first_bias, other_squares
    )
    half = lax.axis_index("dp") % NH
    mine = lax.dynamic_slice_in_dim(weight_sum, half * 4, weight_noise.shape[0], 0)
    weight_grad = (mine + weight_noise) / EXAMPLES
    bias_grad = (bias_sum[: F // 128].reshape(F) + bias_noise) / EXAMPLES
    return (input_t.T, weight_grad, bias_grad)


def solution(mesh):
    placed = (P("dp", "mp"), P(None, "mp"), P("mp"), P("dp", "mp"), P("dp"), P("dp", "mp"), P("mp"))
    return jax.shard_map(
        per_device,
        mesh=mesh,
        in_specs=placed,
        out_specs=(P("dp", "mp"), P("dp", "mp"), P("mp")),
        check_vma=False,
    )
```

time: 78 us -> 68.7 us (0.88)
  the two profiles are of different devices: /device:TPU:2 before, /device:TPU:24 now
where the time goes in v2:
time: 68.7 us; the launch traced here: 68.4 us
  Pallas kernels  63.4 us (92%)
  other arithmetic  2.75 us (4%)
  local copies, waits for them, and re-layouts  1.6 us (2%)
    pallas_call x1, Pallas kernels, fused(): pl.pallas_call(kernel, out_shape=(jax.ShapeDtypeStruct((R, 2 * SEQ), BF16...  63.4 us
    unnamed x5, local copies, waits for them, and re-layouts  1.6 us
    div x1, other arithmetic, per_device(): weight_grad = (mine + weight_noise) / EXAMPLES  1.47 us

profile of v2, /device:TPU:24, one launch (start us, length us, event | category | flops | bytes accessed | tf_op | source)
XLA Modules:
  0.0 68.4 jit_solution(2953053131132236815)
XLA Ops:
  0.6 0.0 copy-start
  0.7 0.0 copy-start.1
  0.7 63.4 %shard_map.94 = (bf16[160,512]{1,0:T(8,128)(2,1)}, f32[24,640]{1,0:T(8,128)}, f32[8,128]{1,0:T(8,128)}) custom-call(bf16[160,512]{1,0:T(8,128)(2,1)} %bitcast.7, bf16[1280,640]{1,0:T(8,128)(2,1)} %w_hbm.1, bf16[512,640]{1,0:T(8,128)(2,1)} %h_hbm.1, f32[640]{0:T(1024)} %bias_hbm.1, f32[2]{0:T(128)} %other_hbm.1), custom_call_target="tpu_custom_call" | custom-call | flops 2516582400 | bytes 3145728 | tf_op jit(solution)/shard_map/pallas_call | solution.py:476
  64.1 0.0 copy-done
  64.1 1.5 %add_multiply_fusion = f32[20,640]{1,0:T(8,128)} fusion(f32[20,640]{1,0:T(8,128)S(1)} %copy-done, f32[24,640]{1,0:T(8,128)} %get-tuple-element.7, s32[]{:T(128)S(6)} %select_n.11), kind=kLoop, calls=%fused_computation | loop fusion | flops 25600 | bytes 153604 | tf_op jit(solution)/shard_map/div | solution.py:521
  65.6 0.0 copy-done.1
  65.6 1.3 %fusion = f32[640]{0:T(1024)} fusion(f32[640]{0:T(1024)S(1)} %copy-done.1, f32[8,128]{1,0:T(8,128)} %get-tuple-element.8), kind=kLoop, calls=%fused_computation.2 | loop fusion | flops 1280 | bytes 7680 | tf_op jit(solution)/shard_map/div | solution.py:522
  66.9 1.6 %copy.11 = bf16[512,160]{0,1:T(8,128)(2,1)} copy(bf16[512,160]{0,1:T(8,128)(2,1)} %bitcast.6) | data formatting | bytes 327680
Async XLA Ops:
  0.6 63.4 %copy-start = (f32[20,640]{1,0:T(8,128)S(1)}, f32[20,640]{1,0:T(8,128)}, u32[]{:S(2)}) copy-start(f32[20,640]{1,0:T(8,128)} %param.12) | copy-start | bytes 153604
  0.7 64.9 %copy-start.1 = (f32[640]{0:T(1024)S(1)}, f32[640]{0:T(1024)}, u32[]{:S(2)}) copy-start(f32[640]{0:T(1024)} %param.13) | copy-start | bytes 7684

commit v3 on v2

--- a/solution.py
+++ b/solution.py
@@ -40,12 +40,12 @@
     x_hbm, w_hbm, h_hbm, bias_hbm, other_hbm,
     ig_ref, wg_ref, bg_ref,
     w, h, bias, other_ref, xg, acc, g, per, nt, bt,
-    bsend, brecv, bown, zsend, zrecv, igacc,
-    wa, ra1, ra2, suma, ya, yra,
+    bsend, brecv, bown, zsend, zrecv, zrel, igacc,
+    wa, ra1, ra2, suma, ya, yra, za, zra, sumz,
     wb, rb, sumb, xb, xrb,
     zs, zsnd, zrcv, bx, by, bz,
-    lsem, ag_s, ag_f, ag_p, ag_r, nsem, nrem, ss_s, ss_r, zz_s, zz_r,
-    a1_s, a1_r, a2_s, a2_r, ya_s, ya_r, b_s, b_r, xb_s, xb_r, h_s, h_r,
+    lsem, ag_s, ag_f, ag_p, ag_r, nsem, nrem, ss_s, ss_r, zz_s, zz_r, zl_s, zl_r,
+    a1_s, a1_r, a2_s, a2_r, ya_s, ya_r, za_s, za_r, b_s, b_r, xb_s, xb_r, h_s, h_r,
     bx_s, bx_r, by_s, by_r, bz_s, bz_r,
 ):
     d, m = lax.axis_index("dp"), lax.axis_index("mp")
@@ -138,15 +138,20 @@
             start(ag_copy(e, i, ag_p.at[e], relay_to), inner)
         start(ag_copy(e, i, ag_f.at[e * 3 + j], sibling))
 
-    def ag_rest(e):
-        for k in range(NZ):
-            i = (z + k) % NZ * NC + 1 - c
-            ag_copy(e, i, ag_s.at[0], sibling).wait_recv()
+    def ag_pair(e, k):
+        i = (z + k) % NZ * NC + 1 - c
+        ag_copy(e, i, ag_s.at[0], sibling).wait_recv()
 
     def pre_act(e):
         acc[...] = lax.dot_general(
             xg[e], w[...], (((0,), (0,)), ((), ())), preferred_element_type=F32
         ) + bias[...].reshape(1, F)
+
+    def pre_act_chip(e, k, start_with):
+        at = rows((z + k) % NZ * (NC * R), NC * R, 64)
+        acc[...] = start_with + lax.dot_general(
+            xg[e, at, :], w[at, :], (((0,), (0,)), ((), ())), preferred_element_type=F32
+        )
 
     def slope(e):
         def step(b, total):
@@ -217,20 +222,46 @@
             at_z(other),
         )
 
+    relay = at_z(jnp.where(z == 0, 1, 2))
+
+    def relay_copy(e, other):
+        return send(zsend.at[e, other], zrel.at[e], zl_s.at[e], zl_r.at[e], relay)
+
     def back_send(e):
         pair_copy(e).wait_recv()
-        for k in (2, 1, 3):
+        for k in (1, 3, 2):
             other = (z + k) % NZ
             zsend[e, other] = (bown[e, other] + brecv[e, other].astype(F32)).astype(BF16)
-            start(z_copy(e, k))
+            if k == 2:
+                start(z_copy(e, k), jnp.logical_not(inner))
+            else:
+                start(z_copy(e, k), jnp.logical_not(far(k)))
+                start(relay_copy(e, other), far(k))
         igacc[e] = bown[e, z] + brecv[e, z].astype(F32)
 
+    def back_relay(e):
+        copy = z_copy(e, 2)
+        other = (z + 2) % NZ
+
+        @pl.when(inner)
+        def _():
+            relay_copy(e, other).wait_recv()
+            zsend[e, other] = (
+                zsend[e, other].astype(F32) + zrel[e].astype(F32)
+            ).astype(BF16)
+
+        start(copy, inner)
+
     def back_take(e):
-        total = igacc[e]
         for k in range(1, NZ):
-            z_copy(e, k).wait_recv()
-            total = total + zrecv[e, k - 1].astype(F32)
-        ig_ref[:, e * SEQ : (e + 1) * SEQ] = total.astype(BF16)
+            comes = jnp.logical_not((z == NZ - 1) & (k == 3) | (z == 0) & (k == 1))
+
+            @pl.when(comes)
+            def _(k=k):
+                z_copy(e, k).wait_recv()
+                igacc[e] += zrecv[e, k - 1].astype(F32)
+
+        ig_ref[:, e * SEQ : (e + 1) * SEQ] = igacc[e].astype(BF16)
 
     ag_start(0)
     ag_start(1)
@@ -238,7 +269,8 @@
         load.wait()
     for j in range(3):
         ag_take(0, j)
-    ag_rest(0)
+    for k in range(NZ):
+        ag_pair(0, k)
     pre_act(0)
     slope(0)
     ag_take(1, 0)
@@ -246,14 +278,22 @@
     norm_start(0)
     ag_take(1, 1)
     back(0)
+    ag_pair(1, 0)
+    pre_act_chip(1, 0, bias[...].reshape(1, F))
+    ag_pair(1, order[0])
+    pre_act_chip(1, order[0], acc[...])
     ag_take(1, 2)
-    ag_rest(1)
-    pre_act(1)
+    ag_pair(1, order[1])
+    pre_act_chip(1, order[1], acc[...])
+    ag_pair(1, order[2])
+    pre_act_chip(1, order[2], acc[...])
     slope(1)
     weight_terms(1)
     norm_start(1)
     back_send(0)
     back(1)
+    back_send(1)
+    back_relay(0)
     norm_wait(0)
     norm_wait(1)
 
@@ -350,6 +390,9 @@
     def pad(value, size):
         return jnp.concatenate([value, jnp.zeros((size - value.shape[0], 128), F32)], axis=0)
 
+    def za_copy(t):
+        return send(za.at[t], zra.at[t], za_s.at[t], za_r.at[t], half_peer)
+
     def a_turn(t):
         for half in range(2):
             value = weighted_a(t, px * 2 + half)
@@ -357,17 +400,29 @@
                 a2_copy(t, way, half).wait_recv()
                 value = value + ra2[t, way, half].astype(F32)
             suma[t, half * R : (half + 1) * R, :] = value
+        za[t] = jnp.concatenate(
+            [suma[t, rows(i * YR + (1 - ph) * 16, 24, 8), :] for i in range(NY)], axis=0
+        ).astype(BF16)
+        start(za_copy(t))
+
+    def a_mid(t):
+        za_copy(t).wait_recv()
+        theirs = zra[t].astype(F32)
+        for i in range(NY):
+            sumz[t, i * 24 : (i + 1) * 24, :] = (
+                suma[t, rows(i * YR + ph * 16, 24, 8), :] + theirs[i * 24 : (i + 1) * 24]
+            )
         for k in (4, 3, 5, 2, 6, 1, 7):
-            block = suma[t, rows((py + k) % NY * YR, YR, 8), :]
-            ya[t, k - 1] = pad(block, 48).astype(BF16)
+            block = sumz[t, rows((py + k) % NY * 24, 24, 8), :]
+            ya[t, k - 1] = pad(block, 32).astype(BF16)
             start(ya_copy(t, k))
 
     def a_take(t):
-        total = suma[t, rows(py * YR, YR, 8), :]
+        total = sumz[t, rows(py * 24, 24, 8), :]
         for k in range(1, NY):
             ya_copy(t, k).wait_recv()
-            total = total + yra[t, k - 1].astype(F32)[0:YR]
-        zs[t * YR : (t + 1) * YR, :] = total
+            total = total + yra[t, k - 1].astype(F32)[0:24]
+        wg_ref[:, t * 128 : (t + 1) * 128] = total
 
     def xb_copy(k):
         return send(xb.at[k - 1], xrb.at[k - 1], xb_s.at[k - 1], xb_r.at[k - 1], at_x(k))
@@ -401,7 +456,7 @@
     a2_sum(1)
     a2_own(2)
     a2_sum(2)
-    back_send(1)
+    back_relay(1)
     for k in range(1, NX):
         bx_copy((px + k) % NX, k).wait_recv()
     by[py] = (bx[0] + bx[1]) + (bx[2] + bx[3])
@@ -414,7 +469,15 @@
     a_turn(1)
     b_step(1, 1)
     a_turn(2)
-
+    a_mid(0)
+    for k in range(1, NY):
+        by_copy((py + k) % NY, k).wait_recv()
+    total = by[0]
+    for i in range(1, NY):
+        total = total + by[i]
+    bz[ph] = total
+    start(bz_copy(ph))
+    a_mid(1)
     for t in range(NB):
         value = weighted_b(t, py)
         for way in range(2):
@@ -424,39 +487,30 @@
     for k in (2, 1, 3):
         xb[k - 1] = pack_b((px + k) % NX).astype(BF16)
         start(xb_copy(k))
-
-    for k in range(1, NY):
-        by_copy((py + k) % NY, k).wait_recv()
-    total = by[0]
-    for i in range(1, NY):
-        total = total + by[i]
-    bz[ph] = total
-    start(bz_copy(ph))
-
-    back_take(0)
-    back_take(1)
-    a_take(0)
-    a_take(1)
+    a_mid(2)
     total = pack_b(px)
     for k in range(1, NX):
         xb_copy(k).wait_recv()
         total = total + xrb[k - 1].astype(F32)
-    zs[NA * YR :, :] = total
-    a_take(2)
+    zs[...] = total
 
     def of_half(half):
-        return [zs[rows(i * YR + half * 16, 24, 8), :] for i in range(F // 128)]
-
-    zsnd[...] = pad(jnp.concatenate(of_half(1 - ph), axis=0), 128).astype(BF16)
+        return [zs[rows(t * YR + half * 16, 24, 8), :] for t in range(NB)]
+
+    zsnd[...] = jnp.concatenate(of_half(1 - ph), axis=0).astype(BF16)
     half_copy = send(zsnd, zrcv, h_s.at[0], h_r.at[0], half_peer)
     start(half_copy)
+    back_take(0)
+    back_take(1)
     bz_copy(1 - ph).wait_recv()
     bg_ref[...] = bz[0] + bz[1]
+    for t in range(NA):
+        a_take(t)
     mine = of_half(ph)
     half_copy.wait_recv()
     theirs = zrcv[...].astype(F32)
-    for i in range(F // 128):
-        wg_ref[:, i * 128 : (i + 1) * 128] = mine[i] + theirs[i * 24 : (i + 1) * 24]
+    for t in range(NB):
+        wg_ref[:, (NA + t) * 128 : (NA + t + 1) * 128] = mine[t] + theirs[t * 24 : (t + 1) * 24]
 
     for copy, when in pending:
         if when is None:
@@ -487,17 +541,18 @@
             buf((2, D, SEQ)), buf((SEQ, F), F32), buf((2, SEQ, F)),
             buf((2, D, F), F32), buf((2, N_MP, 8, 128), F32), buf((2, 8, 128), F32),
             buf((2, NZ, R, SEQ)), buf((2, NZ, R, SEQ)), buf((2, NZ, R, SEQ), F32),
-            buf((2, NZ, R, SEQ)), buf((2, NZ - 1, R, SEQ)), buf((2, R, SEQ), F32),
+            buf((2, NZ, R, SEQ)), buf((2, NZ - 1, R, SEQ)), buf((2, R, SEQ)), buf((2, R, SEQ), F32),
             buf((NA, 8, R, 128)), buf((NA, 2, R, 128)), buf((NA, 2, 2, R, 128)),
-            buf((NA, XR, 128), F32), buf((NA, NY - 1, 48, 128)), buf((NA, NY - 1, 48, 128)),
+            buf((NA, XR, 128), F32), buf((NA, NY - 1, 32, 128)), buf((NA, NY - 1, 32, 128)),
+            buf((NA, 192, 128)), buf((NA, 192, 128)), buf((NA, 192, 128), F32),
             buf((NB, NY, 160, 128)), buf((NB, 2, 4, 160, 128)), buf((NB, 160, 128), F32),
             buf((NX - 1, 80, 128)), buf((NX - 1, 80, 128)),
-            buf((200, 128), F32), buf((128, 128)), buf((128, 128)),
+            buf((NB * YR, 128), F32), buf((NB * 24, 128)), buf((NB * 24, 128)),
             buf((NX, 8, 128), F32), buf((NY, 8, 128), F32), buf((NH, 8, 128), F32),
             dma((6,)), dma((8,)), dma((6,)), dma((2,)), dma((16,)),
-            dma((16,)), dma((16,)), dma((2,)), dma((2,)), dma((6,)), dma((6,)),
+            dma((16,)), dma((16,)), dma((2,)), dma((2,)), dma((6,)), dma((6,)), dma((2,)), dma((2,)),
             dma((NA * 2,)), dma((NA * 2,)), dma((NA * 4,)), dma((NA * 4,)),
-            dma((NA * 7,)), dma((NA * 7,)),
+            dma((NA * 7,)), dma((NA * 7,)), dma((NA,)), dma((NA,)),
             dma((NB * 8,)), dma((NB * 8,)), dma((3,)), dma((3,)), dma((1,)), dma((1,)),
             dma((NX,)), dma((NX,)), dma((NY,)), dma((NY,)), dma((1,)), dma((NH,)),
         ],

time: 68.7 us -> 69.7 us (1.015)
  the two profiles are of different devices: /device:TPU:24 before, /device:TPU:64 now
where the time goes in v3:
time: 69.7 us; the launch traced here: 69.4 us
  Pallas kernels  64.4 us (92%)
  other arithmetic  2.75 us (4%)
  local copies, waits for them, and re-layouts  1.6 us (2%)
    pallas_call x1, Pallas kernels, fused(): pl.pallas_call(kernel, out_shape=(jax.ShapeDtypeStruct((R, 2 * SEQ), BF16...  64.4 us
    unnamed x5, local copies, waits for them, and re-layouts  1.6 us
    div x1, other arithmetic, per_device(): weight_grad = (mine + weight_noise) / EXAMPLES  1.47 us

profile of v3, /device:TPU:64, one launch (start us, length us, event | category | flops | bytes accessed | tf_op | source)
XLA Modules:
  0.0 69.4 jit_solution(4016462427410500581)
XLA Ops:
  0.6 0.0 copy-start
  0.7 0.0 copy-start.1
  0.7 64.4 %shard_map.94 = (bf16[160,512]{1,0:T(8,128)(2,1)}, f32[24,640]{1,0:T(8,128)}, f32[8,128]{1,0:T(8,128)}) custom-call(bf16[160,512]{1,0:T(8,128)(2,1)} %bitcast.7, bf16[1280,640]{1,0:T(8,128)(2,1)} %w_hbm.1, bf16[512,640]{1,0:T(8,128)(2,1)} %h_hbm.1, f32[640]{0:T(1024)} %bias_hbm.1, f32[2]{0:T(128)} %other_hbm.1), custom_call_target="tpu_custom_call" | custom-call | flops 2516582400 | bytes 3145728 | tf_op jit(solution)/shard_map/pallas_call | solution.py:530
  65.1 0.0 copy-done
  65.1 1.5 %add_multiply_fusion = f32[20,640]{1,0:T(8,128)} fusion(f32[20,640]{1,0:T(8,128)S(1)} %copy-done, f32[24,640]{1,0:T(8,128)} %get-tuple-element.7, s32[]{:T(128)S(6)} %select_n.11), kind=kLoop, calls=%fused_computation | loop fusion | flops 25600 | bytes 153604 | tf_op jit(solution)/shard_map/div | solution.py:576
  66.6 0.0 copy-done.1
  66.6 1.3 %fusion = f32[640]{0:T(1024)} fusion(f32[640]{0:T(1024)S(1)} %copy-done.1, f32[8,128]{1,0:T(8,128)} %get-tuple-element.8), kind=kLoop, calls=%fused_computation.2 | loop fusion | flops 1280 | bytes 7680 | tf_op jit(solution)/shard_map/div | solution.py:577
  67.8 1.6 %copy.11 = bf16[512,160]{0,1:T(8,128)(2,1)} copy(bf16[512,160]{0,1:T(8,128)(2,1)} %bitcast.6) | data formatting | bytes 327680
Async XLA Ops:
  0.6 64.4 %copy-start = (f32[20,640]{1,0:T(8,128)S(1)}, f32[20,640]{1,0:T(8,128)}, u32[]{:S(2)}) copy-start(f32[20,640]{1,0:T(8,128)} %param.12) | copy-start | bytes 153604
  0.7 65.9 %copy-start.1 = (f32[640]{0:T(1024)S(1)}, f32[640]{0:T(1024)}, u32[]{:S(2)}) copy-start(f32[640]{0:T(1024)} %param.13) | copy-start | bytes 7684

commit v4 on v3

--- a/solution.py
+++ b/solution.py
@@ -40,11 +40,11 @@
     x_hbm, w_hbm, h_hbm, bias_hbm, other_hbm,
     ig_ref, wg_ref, bg_ref,
     w, h, bias, other_ref, xg, acc, g, per, nt, bt,
-    bsend, brecv, bown, zsend, zrecv, zrel, igacc,
+    bsend, brecv, bown, zsend, zrecv, igacc,
     wa, ra1, ra2, suma, ya, yra, za, zra, sumz,
     wb, rb, sumb, xb, xrb,
     zs, zsnd, zrcv, bx, by, bz,
-    lsem, ag_s, ag_f, ag_p, ag_r, nsem, nrem, ss_s, ss_r, zz_s, zz_r, zl_s, zl_r,
+    lsem, ag_s, ag_f, ag_p, ag_r, nsem, nrem, ss_s, ss_r, zz_s, zz_r,
     a1_s, a1_r, a2_s, a2_r, ya_s, ya_r, za_s, za_r, b_s, b_r, xb_s, xb_r, h_s, h_r,
     bx_s, bx_r, by_s, by_r, bz_s, bz_r,
 ):
@@ -222,44 +222,18 @@
             at_z(other),
         )
 
-    relay = at_z(jnp.where(z == 0, 1, 2))
-
-    def relay_copy(e, other):
-        return send(zsend.at[e, other], zrel.at[e], zl_s.at[e], zl_r.at[e], relay)
-
     def back_send(e):
         pair_copy(e).wait_recv()
-        for k in (1, 3, 2):
+        for k in (2, 1, 3):
             other = (z + k) % NZ
             zsend[e, other] = (bown[e, other] + brecv[e, other].astype(F32)).astype(BF16)
-            if k == 2:
-                start(z_copy(e, k), jnp.logical_not(inner))
-            else:
-                start(z_copy(e, k), jnp.logical_not(far(k)))
-                start(relay_copy(e, other), far(k))
+            start(z_copy(e, k))
         igacc[e] = bown[e, z] + brecv[e, z].astype(F32)
-
-    def back_relay(e):
-        copy = z_copy(e, 2)
-        other = (z + 2) % NZ
-
-        @pl.when(inner)
-        def _():
-            relay_copy(e, other).wait_recv()
-            zsend[e, other] = (
-                zsend[e, other].astype(F32) + zrel[e].astype(F32)
-            ).astype(BF16)
-
-        start(copy, inner)
 
     def back_take(e):
         for k in range(1, NZ):
-            comes = jnp.logical_not((z == NZ - 1) & (k == 3) | (z == 0) & (k == 1))
-
-            @pl.when(comes)
-            def _(k=k):
-                z_copy(e, k).wait_recv()
-                igacc[e] += zrecv[e, k - 1].astype(F32)
+            z_copy(e, k).wait_recv()
+            igacc[e] += zrecv[e, k - 1].astype(F32)
 
         ig_ref[:, e * SEQ : (e + 1) * SEQ] = igacc[e].astype(BF16)
 
@@ -293,7 +267,6 @@
     back_send(0)
     back(1)
     back_send(1)
-    back_relay(0)
     norm_wait(0)
     norm_wait(1)
 
@@ -456,7 +429,6 @@
     a2_sum(1)
     a2_own(2)
     a2_sum(2)
-    back_relay(1)
     for k in range(1, NX):
         bx_copy((px + k) % NX, k).wait_recv()
     by[py] = (bx[0] + bx[1]) + (bx[2] + bx[3])
@@ -541,7 +513,7 @@
             buf((2, D, SEQ)), buf((SEQ, F), F32), buf((2, SEQ, F)),
             buf((2, D, F), F32), buf((2, N_MP, 8, 128), F32), buf((2, 8, 128), F32),
             buf((2, NZ, R, SEQ)), buf((2, NZ, R, SEQ)), buf((2, NZ, R, SEQ), F32),
-            buf((2, NZ, R, SEQ)), buf((2, NZ - 1, R, SEQ)), buf((2, R, SEQ)), buf((2, R, SEQ), F32),
+            buf((2, NZ, R, SEQ)), buf((2, NZ - 1, R, SEQ)), buf((2, R, SEQ), F32),
             buf((NA, 8, R, 128)), buf((NA, 2, R, 128)), buf((NA, 2, 2, R, 128)),
             buf((NA, XR, 128), F32), buf((NA, NY - 1, 32, 128)), buf((NA, NY - 1, 32, 128)),
             buf((NA, 192, 128)), buf((NA, 192, 128)), buf((NA, 192, 128), F32),
@@ -550,7 +522,7 @@
             buf((NB * YR, 128), F32), buf((NB * 24, 128)), buf((NB * 24, 128)),
             buf((NX, 8, 128), F32), buf((NY, 8, 128), F32), buf((NH, 8, 128), F32),
             dma((6,)), dma((8,)), dma((6,)), dma((2,)), dma((16,)),
-            dma((16,)), dma((16,)), dma((2,)), dma((2,)), dma((6,)), dma((6,)), dma((2,)), dma((2,)),
+            dma((16,)), dma((16,)), dma((2,)), dma((2,)), dma((6,)), dma((6,)),
             dma((NA * 2,)), dma((NA * 2,)), dma((NA * 4,)), dma((NA * 4,)),
             dma((NA * 7,)), dma((NA * 7,)), dma((NA,)), dma((NA,)),
             dma((NB * 8,)), dma((NB * 8,)), dma((3,)), dma((3,)), dma((1,)), dma((1,)),

time: 69.7 us -> 66.3 us (0.951)
  the two profiles are of different devices: /device:TPU:64 before, /device:TPU:24 now
where the time goes in v4:
time: 66.3 us; the launch traced here: 66.1 us
  Pallas kernels  61 us (92%)
  other arithmetic  2.75 us (4%)
  local copies, waits for them, and re-layouts  1.6 us (2%)
  between operations  0.68 us (1%)
    pallas_call x1, Pallas kernels, fused(): pl.pallas_call(kernel, out_shape=(jax.ShapeDtypeStruct((R, 2 * SEQ), BF16...  61 us
    unnamed x5, local copies, waits for them, and re-layouts  1.6 us
    div x1, other arithmetic, per_device(): weight_grad = (mine + weight_noise) / EXAMPLES  1.47 us

profile of v4, /device:TPU:24, one launch (start us, length us, event | category | flops | bytes accessed | tf_op | source)
XLA Modules:
  0.0 66.1 jit_solution(4349428688087839204)
XLA Ops:
  0.6 0.0 copy-start
  0.7 0.0 copy-start.1
  0.7 61.0 %shard_map.94 = (bf16[160,512]{1,0:T(8,128)(2,1)}, f32[24,640]{1,0:T(8,128)}, f32[8,128]{1,0:T(8,128)}) custom-call(bf16[160,512]{1,0:T(8,128)(2,1)} %bitcast.7, bf16[1280,640]{1,0:T(8,128)(2,1)} %w_hbm.1, bf16[512,640]{1,0:T(8,128)(2,1)} %h_hbm.1, f32[640]{0:T(1024)} %bias_hbm.1, f32[2]{0:T(128)} %other_hbm.1), custom_call_target="tpu_custom_call" | custom-call | flops 2516582400 | bytes 3145728 | tf_op jit(solution)/shard_map/pallas_call | solution.py:502
  61.7 0.0 copy-done
  61.7 1.5 %add_multiply_fusion = f32[20,640]{1,0:T(8,128)} fusion(f32[20,640]{1,0:T(8,128)S(1)} %copy-done, f32[24,640]{1,0:T(8,128)} %get-tuple-element.7, s32[]{:T(128)S(6)} %select_n.11), kind=kLoop, calls=%fused_computation | loop fusion | flops 25600 | bytes 153604 | tf_op jit(solution)/shard_map/div | solution.py:548
  63.2 0.0 copy-done.1
  63.2 1.3 %fusion = f32[640]{0:T(1024)} fusion(f32[640]{0:T(1024)S(1)} %copy-done.1, f32[8,128]{1,0:T(8,128)} %get-tuple-element.8), kind=kLoop, calls=%fused_computation.2 | loop fusion | flops 1280 | bytes 7680 | tf_op jit(solution)/shard_map/div | solution.py:549
  64.5 1.6 %copy.11 = bf16[512,160]{0,1:T(8,128)(2,1)} copy(bf16[512,160]{0,1:T(8,128)(2,1)} %bitcast.6) | data formatting | bytes 327680
Async XLA Ops:
  0.6 61.1 %copy-start = (f32[20,640]{1,0:T(8,128)S(1)}, f32[20,640]{1,0:T(8,128)}, u32[]{:S(2)}) copy-start(f32[20,640]{1,0:T(8,128)} %param.12) | copy-start | bytes 153604
  0.7 62.5 %copy-start.1 = (f32[640]{0:T(1024)S(1)}, f32[640]{0:T(1024)}, u32[]{:S(2)}) copy-start(f32[640]{0:T(1024)} %param.13) | copy-start | bytes 7684

commit v5 on v4

--- a/solution.py
+++ b/solution.py
@@ -41,11 +41,11 @@
     ig_ref, wg_ref, bg_ref,
     w, h, bias, other_ref, xg, acc, g, per, nt, bt,
     bsend, brecv, bown, zsend, zrecv, igacc,
-    wa, ra1, ra2, suma, ya, yra, za, zra, sumz,
+    wa, ra1, ra2, ua, ub, rub, fs, frx, fry, suma, ya, yra, za, zra, sumz,
     wb, rb, sumb, xb, xrb,
-    zs, zsnd, zrcv, bx, by, bz,
+    bx, by, bz,
     lsem, ag_s, ag_f, ag_p, ag_r, nsem, nrem, ss_s, ss_r, zz_s, zz_r,
-    a1_s, a1_r, a2_s, a2_r, ya_s, ya_r, za_s, za_r, b_s, b_r, xb_s, xb_r, h_s, h_r,
+    a1_s, a1_r, ub_s, ub_r, fx_s, fx_r, fy_s, fy_r, a2_s, a2_r, ya_s, ya_r, za_s, za_r, b_s, b_r, xb_s, xb_r,
     bx_s, bx_r, by_s, by_r, bz_s, bz_r,
 ):
     d, m = lax.axis_index("dp"), lax.axis_index("mp")
@@ -62,6 +62,9 @@
     def at_y(k):
         return ((px * NY + (py + k) % NY) * NH + ph, m)
 
+    def at_xh(k, other):
+        return (((px + k) % NX * NY + py) * NH + (ph + other) % NH, m)
+
     half_peer = (d + 1 - 2 * ph, m)
 
     def send(src, dst, ssem, rsem, device):
@@ -102,13 +105,14 @@
         greet((d, (m + k) % N_MP))
     for k in range(1, NX):
         greet(at_x(k))
+        greet(at_xh(k, 1))
     for k in range(1, NY):
         greet(at_y(k))
     greet(half_peer)
 
     load_x[0].wait()
     load_x[1].wait()
-    pl.semaphore_wait(barrier, N_MP - 1 + NX - 1 + NY - 1 + 1)
+    pl.semaphore_wait(barrier, N_MP - 1 + 2 * (NX - 1) + NY - 1 + 1)
 
     def slot(e, i):
         return xg.at[e, rows(i * R, R, 32), :]
@@ -236,6 +240,46 @@
             igacc[e] += zrecv[e, k - 1].astype(F32)
 
         ig_ref[:, e * SEQ : (e + 1) * SEQ] = igacc[e].astype(BF16)
+
+    step_x = (1, NX - 1)
+    step_y = (1, NY - 1)
+
+    def index_a(k, half):
+        return (px + k) % NX * 2 + half
+
+    def index_b(way, k):
+        return (py + (k if way == 0 else NY - k)) % NY
+
+    def ua_copy(t, way, e):
+        n = (t * 2 + way) * 2 + e
+        return send(
+            ua.at[t, way, e], ra1.at[t, way, e], a1_s.at[n], a1_r.at[n], at_x(step_x[way])
+        )
+
+    def ub_copy(t, way, e):
+        n = (t * 2 + way) * 2 + e
+        return send(
+            ub.at[t, way, e], rub.at[t, way, e], ub_s.at[n], ub_r.at[n], at_y(step_y[way])
+        )
+
+    def early(e):
+        for t in range(NA):
+            for way in range(2):
+                at = rows(index_a(2, way) * R, R, 32)
+                ua[t, way, e] = per[e, at, t * 128 : (t + 1) * 128].astype(BF16)
+                start(ua_copy(t, way, e))
+        owner = (py + 4) % NY
+        for t in range(NB):
+            columns = slice((NA + t) * 128, (NA + t + 1) * 128)
+            for way in range(2):
+                ub[t, way, e] = jnp.concatenate(
+                    [
+                        per[e, rows(i * XR + owner * YR, YR, 8), columns]
+                        for i in (2 * way, 2 * way + 1)
+                    ],
+                    axis=0,
+                ).astype(BF16)
+                start(ub_copy(t, way, e))
 
     ag_start(0)
     ag_start(1)
@@ -250,6 +294,7 @@
     ag_take(1, 0)
     weight_terms(0)
     norm_start(0)
+    early(0)
     ag_take(1, 1)
     back(0)
     ag_pair(1, 0)
@@ -264,6 +309,7 @@
     slope(1)
     weight_terms(1)
     norm_start(1)
+    early(1)
     back_send(0)
     back(1)
     back_send(1)
@@ -291,21 +337,6 @@
             [weighted(NA + t, i * XR + owner * YR, YR, 8) for i in range(NX)], axis=0
         )
 
-    step_x = (1, NX - 1)
-    step_y = (1, NY - 1)
-
-    def index_a(k, half):
-        return (px + k) % NX * 2 + half
-
-    def index_b(way, k):
-        return (py + (k if way == 0 else NY - k)) % NY
-
-    def a1_copy(t, way):
-        return send(
-            wa.at[t, index_a(2, way)], ra1.at[t, way], a1_s.at[t * 2 + way], a1_r.at[t * 2 + way],
-            at_x(step_x[way]),
-        )
-
     def a2_copy(t, way, half):
         n = (t * 2 + way) * 2 + half
         return send(
@@ -313,24 +344,39 @@
             at_x(step_x[way]),
         )
 
-    def part_b(way, k):
-        return (slice(0, 80), slice(80, 160))[way] if k == 4 else slice(0, 160)
-
     def b_copy(t, way, k):
-        n, part = (t * 2 + way) * 4 + k - 1, part_b(way, k)
+        n, owner = (t * 2 + way) * 3 + k - 1, index_b(way, k)
         return send(
-            wb.at[t, index_b(way, k), part], rb.at[t, way, k - 1, part], b_s.at[n], b_r.at[n],
-            at_y(step_y[way]),
+            wb.at[t, owner], rb.at[t, way, k - 1], b_s.at[n], b_r.at[n], at_y(step_y[way])
+        )
+
+    def fx_copy(way):
+        return send(fs, frx.at[way], fx_s.at[way], fx_r.at[way], at_x(step_x[way]))
+
+    def fy_copy(way):
+        return send(fs, fry.at[way], fy_s.at[way], fy_r.at[way], at_y(step_y[way]))
+
+    def scaled(factor, first_part, second_part):
+        return (
+            factor[0:1] * first_part.astype(F32) + factor[1:2] * second_part.astype(F32)
         )
 
     def b_step(t, k):
         for way in range(2):
             owner = index_b(way, k)
-            b_copy(t, way, k + 1).wait_recv()
-            part = part_b(way, k + 1)
-            wb[t, owner, part] = (
-                wb[t, owner, part].astype(F32) + rb[t, way, k, part].astype(F32)
-            ).astype(BF16)
+            value = weighted_b(t, owner)
+            if k == 3:
+                for e in range(2):
+                    ub_copy(t, way, e).wait_recv()
+                more = scaled(fry[way], rub[t, way, 0], rub[t, way, 1])
+                low, high = value[0:80], value[80:160]
+                value = jnp.concatenate(
+                    [low + more, high] if way == 0 else [low, high + more], axis=0
+                )
+            else:
+                b_copy(t, way, k + 1).wait_recv()
+                value = value + rb[t, way, k].astype(F32)
+            wb[t, owner] = value.astype(BF16)
             start(b_copy(t, way, k))
 
     def bx_copy(i, k):
@@ -352,8 +398,10 @@
         for way in range(2):
             i = index_a(step_x[way], way)
             value = weighted_a(t, i)
-            a1_copy(t, way).wait_recv()
-            wa[t, i] = (value + ra1[t, way].astype(F32)).astype(BF16)
+            for e in range(2):
+                ua_copy(t, way, e).wait_recv()
+            value = value + scaled(frx[way], ra1[t, way, 0], ra1[t, way, 1])
+            wa[t, i] = value.astype(BF16)
             start(a2_copy(t, way, way))
 
     def ya_copy(t, k):
@@ -397,51 +445,48 @@
             total = total + yra[t, k - 1].astype(F32)[0:24]
         wg_ref[:, t * 128 : (t + 1) * 128] = total
 
-    def xb_copy(k):
-        return send(xb.at[k - 1], xrb.at[k - 1], xb_s.at[k - 1], xb_r.at[k - 1], at_x(k))
-
-    def pack_b(owner):
-        at = rows(owner * YR, YR, 8)
+    others = [(k, j) for k in (2, 1, 3, 0) for j in (1, 0) if (k, j) != (0, 0)]
+
+    def xb_copy(k, j):
+        n = k * 2 + j - 1
+        return send(xb.at[n], xrb.at[n], xb_s.at[n], xb_r.at[n], at_xh(k, j))
+
+    def pack_b(owner, half):
+        at = rows(owner * YR + half * 16, 24, 8)
         return jnp.concatenate([sumb[t, at, :] for t in range(NB)], axis=0)
 
+    fs[...] = jnp.broadcast_to(f0, (8, 128))
+    fs[1:2, :] = f1
+    for way in range(2):
+        start(fy_copy(way))
+        start(fx_copy(way))
     for t in range(NA):
-        for way in range(2):
-            i = index_a(2, way)
-            wa[t, i] = weighted_a(t, i).astype(BF16)
-            start(a1_copy(t, way))
-    for t in range(NB):
-        owner = (py + 4) % NY
-        wb[t, owner] = weighted_b(t, owner).astype(BF16)
-        for way in range(2):
-            start(b_copy(t, way, 4))
-    a2_own(0)
+        a2_own(t)
     bx[px] = f0 * bt[0] + f1 * bt[1]
     for k in range(1, NX):
         start(bx_copy(px, k))
-    for k in (3, 5, 2, 6, 1, 7):
-        owner = (py + k) % NY
-        for t in range(NB):
-            wb[t, owner] = weighted_b(t, owner).astype(BF16)
+    for way in range(2):
+        fy_copy(way).wait_recv()
     for t in range(NB):
         b_step(t, 3)
-    a2_sum(0)
-    a2_own(1)
-    a2_sum(1)
-    a2_own(2)
-    a2_sum(2)
+    for way in range(2):
+        fx_copy(way).wait_recv()
+    for t in range(NA):
+        a2_sum(t)
     for k in range(1, NX):
         bx_copy((px + k) % NX, k).wait_recv()
     by[py] = (bx[0] + bx[1]) + (bx[2] + bx[3])
     for k in range(1, NY):
         start(by_copy(py, k))
-    for t in range(NB):
-        b_step(t, 2)
+    b_step(0, 2)
     a_turn(0)
+    b_step(1, 2)
+    a_turn(1)
+    a_turn(2)
     b_step(0, 1)
-    a_turn(1)
+    a_mid(0)
     b_step(1, 1)
-    a_turn(2)
-    a_mid(0)
+    a_mid(1)
     for k in range(1, NY):
         by_copy((py + k) % NY, k).wait_recv()
     total = by[0]
@@ -449,40 +494,28 @@
         total = total + by[i]
     bz[ph] = total
     start(bz_copy(ph))
-    a_mid(1)
+    a_mid(2)
     for t in range(NB):
         value = weighted_b(t, py)
         for way in range(2):
             b_copy(t, way, 1).wait_recv()
             value = value + rb[t, way, 0].astype(F32)
         sumb[t] = value
-    for k in (2, 1, 3):
-        xb[k - 1] = pack_b((px + k) % NX).astype(BF16)
-        start(xb_copy(k))
-    a_mid(2)
-    total = pack_b(px)
-    for k in range(1, NX):
-        xb_copy(k).wait_recv()
-        total = total + xrb[k - 1].astype(F32)
-    zs[...] = total
-
-    def of_half(half):
-        return [zs[rows(t * YR + half * 16, 24, 8), :] for t in range(NB)]
-
-    zsnd[...] = jnp.concatenate(of_half(1 - ph), axis=0).astype(BF16)
-    half_copy = send(zsnd, zrcv, h_s.at[0], h_r.at[0], half_peer)
-    start(half_copy)
+    for k, j in others:
+        xb[k * 2 + j - 1] = pack_b((px + k) % NX, (ph + j) % NH).astype(BF16)
+        start(xb_copy(k, j))
     back_take(0)
     back_take(1)
     bz_copy(1 - ph).wait_recv()
     bg_ref[...] = bz[0] + bz[1]
     for t in range(NA):
         a_take(t)
-    mine = of_half(ph)
-    half_copy.wait_recv()
-    theirs = zrcv[...].astype(F32)
+    total = pack_b(px, ph)
+    for k, j in others:
+        xb_copy(k, j).wait_recv()
+        total = total + xrb[k * 2 + j - 1].astype(F32)
     for t in range(NB):
-        wg_ref[:, (NA + t) * 128 : (NA + t + 1) * 128] = mine[t] + theirs[t * 24 : (t + 1) * 24]
+        wg_ref[:, (NA + t) * 128 : (NA + t + 1) * 128] = total[t * 24 : (t + 1) * 24]
 
     for copy, when in pending:
         if when is None:
@@ -514,18 +547,20 @@
             buf((2, D, F), F32), buf((2, N_MP, 8, 128), F32), buf((2, 8, 128), F32),
             buf((2, NZ, R, SEQ)), buf((2, NZ, R, SEQ)), buf((2, NZ, R, SEQ), F32),
             buf((2, NZ, R, SEQ)), buf((2, NZ - 1, R, SEQ)), buf((2, R, SEQ), F32),
-            buf((NA, 8, R, 128)), buf((NA, 2, R, 128)), buf((NA, 2, 2, R, 128)),
+            buf((NA, 8, R, 128)), buf((NA, 2, 2, R, 128)), buf((NA, 2, 2, R, 128)),
+            buf((NA, 2, 2, R, 128)), buf((NB, 2, 2, 80, 128)), buf((NB, 2, 2, 80, 128)),
+            buf((8, 128), F32), buf((2, 8, 128), F32), buf((2, 8, 128), F32),
             buf((NA, XR, 128), F32), buf((NA, NY - 1, 32, 128)), buf((NA, NY - 1, 32, 128)),
             buf((NA, 192, 128)), buf((NA, 192, 128)), buf((NA, 192, 128), F32),
-            buf((NB, NY, 160, 128)), buf((NB, 2, 4, 160, 128)), buf((NB, 160, 128), F32),
-            buf((NX - 1, 80, 128)), buf((NX - 1, 80, 128)),
-            buf((NB * YR, 128), F32), buf((NB * 24, 128)), buf((NB * 24, 128)),
+            buf((NB, NY, 160, 128)), buf((NB, 2, 3, 160, 128)), buf((NB, 160, 128), F32),
+            buf((7, NB * 24, 128)), buf((7, NB * 24, 128)),
             buf((NX, 8, 128), F32), buf((NY, 8, 128), F32), buf((NH, 8, 128), F32),
             dma((6,)), dma((8,)), dma((6,)), dma((2,)), dma((16,)),
             dma((16,)), dma((16,)), dma((2,)), dma((2,)), dma((6,)), dma((6,)),
-            dma((NA * 2,)), dma((NA * 2,)), dma((NA * 4,)), dma((NA * 4,)),
+            dma((NA * 4,)), dma((NA * 4,)), dma((NB * 4,)), dma((NB * 4,)),
+            dma((2,)), dma((2,)), dma((2,)), dma((2,)), dma((NA * 4,)), dma((NA * 4,)),
             dma((NA * 7,)), dma((NA * 7,)), dma((NA,)), dma((NA,)),
-            dma((NB * 8,)), dma((NB * 8,)), dma((3,)), dma((3,)), dma((1,)), dma((1,)),
+            dma((NB * 6,)), dma((NB * 6,)), dma((7,)), dma((7,)),
             dma((NX,)), dma((NX,)), dma((NY,)), dma((NY,)), dma((1,)), dma((NH,)),
         ],
         compiler_params=pltpu.CompilerParams(

time: 66.3 us -> 69.3 us (1.045)
  the two profiles are of different devices: /device:TPU:24 before, /device:TPU:64 now
where the time goes in v5:
time: 69.3 us; the launch traced here: 68.9 us
  Pallas kernels  63.9 us (92%)
  other arithmetic  2.75 us (4%)
  local copies, waits for them, and re-layouts  1.6 us (2%)
    pallas_call x1, Pallas kernels, fused(): pl.pallas_call(kernel, out_shape=(jax.ShapeDtypeStruct((R, 2 * SEQ), BF16...  63.9 us
    unnamed x5, local copies, waits for them, and re-layouts  1.6 us
    div x1, other arithmetic, per_device(): weight_grad = (mine + weight_noise) / EXAMPLES  1.47 us

profile of v5, /device:TPU:64, one launch (start us, length us, event | category | flops | bytes accessed | tf_op | source)
XLA Modules:
  0.0 68.9 jit_solution(13465238703554261860)
XLA Ops:
  0.6 0.0 copy-start
  0.7 0.0 copy-start.1
  0.7 63.9 %shard_map.94 = (bf16[160,512]{1,0:T(8,128)(2,1)}, f32[24,640]{1,0:T(8,128)}, f32[8,128]{1,0:T(8,128)}) custom-call(bf16[160,512]{1,0:T(8,128)(2,1)} %bitcast.7, bf16[1280,640]{1,0:T(8,128)(2,1)} %w_hbm.1, bf16[512,640]{1,0:T(8,128)(2,1)} %h_hbm.1, f32[640]{0:T(1024)} %bias_hbm.1, f32[2]{0:T(128)} %other_hbm.1), custom_call_target="tpu_custom_call" | custom-call | flops 2516582400 | bytes 3145728 | tf_op jit(solution)/shard_map/pallas_call | solution.py:535
  64.6 0.0 copy-done
  64.6 1.5 %add_multiply_fusion = f32[20,640]{1,0:T(8,128)} fusion(f32[20,640]{1,0:T(8,128)S(1)} %copy-done, f32[24,640]{1,0:T(8,128)} %get-tuple-element.7, s32[]{:T(128)S(6)} %select_n.11), kind=kLoop, calls=%fused_computation | loop fusion | flops 25600 | bytes 153604 | tf_op jit(solution)/shard_map/div | solution.py:583
  66.1 0.0 copy-done.1
  66.1 1.3 %fusion = f32[640]{0:T(1024)} fusion(f32[640]{0:T(1024)S(1)} %copy-done.1, f32[8,128]{1,0:T(8,128)} %get-tuple-element.8), kind=kLoop, calls=%fused_computation.2 | loop fusion | flops 1280 | bytes 7680 | tf_op jit(solution)/shard_map/div | solution.py:584
  67.3 1.6 %copy.11 = bf16[512,160]{0,1:T(8,128)(2,1)} copy(bf16[512,160]{0,1:T(8,128)(2,1)} %bitcast.6) | data formatting | bytes 327680
Async XLA Ops:
  0.6 63.9 %copy-start = (f32[20,640]{1,0:T(8,128)S(1)}, f32[20,640]{1,0:T(8,128)}, u32[]{:S(2)}) copy-start(f32[20,640]{1,0:T(8,128)} %param.12) | copy-start | bytes 153604
  0.7 65.4 %copy-start.1 = (f32[640]{0:T(1024)S(1)}, f32[640]{0:T(1024)}, u32[]{:S(2)}) copy-start(f32[640]{0:T(1024)} %param.13) | copy-start | bytes 7684

commit v6 on v5

--- a/solution.py
+++ b/solution.py
@@ -479,14 +479,13 @@
     for k in range(1, NY):
         start(by_copy(py, k))
     b_step(0, 2)
+    b_step(1, 2)
     a_turn(0)
-    b_step(1, 2)
     a_turn(1)
     a_turn(2)
     b_step(0, 1)
+    b_step(1, 1)
     a_mid(0)
-    b_step(1, 1)
-    a_mid(1)
     for k in range(1, NY):
         by_copy((py + k) % NY, k).wait_recv()
     total = by[0]
@@ -494,7 +493,7 @@
         total = total + by[i]
     bz[ph] = total
     start(bz_copy(ph))
-    a_mid(2)
+    a_mid(1)
     for t in range(NB):
         value = weighted_b(t, py)
         for way in range(2):
@@ -504,6 +503,7 @@
     for k, j in others:
         xb[k * 2 + j - 1] = pack_b((px + k) % NX, (ph + j) % NH).astype(BF16)
         start(xb_copy(k, j))
+    a_mid(2)
     back_take(0)
     back_take(1)
     bz_copy(1 - ph).wait_recv()

time: 69.3 us -> 65.8 us (0.949)
  Pallas kernels: 63.9 us -> 60.5 us
    pallas_call x1, Pallas kernels: 63.9 us -> 60.5 us  [fused(): pl.pallas_call(kernel, out_shape=(jax.ShapeDtypeStruct((R, 2 * SEQ), BF16...]
where the time goes in v6:
time: 65.8 us; the launch traced here: 65.5 us
  Pallas kernels  60.5 us (92%)
  other arithmetic  2.75 us (4%)
  local copies, waits for them, and re-layouts  1.6 us (2%)
  between operations  0.68 us (1%)
    pallas_call x1, Pallas kernels, fused(): pl.pallas_call(kernel, out_shape=(jax.ShapeDtypeStruct((R, 2 * SEQ), BF16...  60.5 us
    unnamed x5, local copies, waits for them, and re-layouts  1.6 us
    div x1, other arithmetic, per_device(): weight_grad = (mine + weight_noise) / EXAMPLES  1.47 us

profile of v6, /device:TPU:64, one launch (start us, length us, event | category | flops | bytes accessed | tf_op | source)
XLA Modules:
  0.0 65.5 jit_solution(17581507564116383539)
XLA Ops:
  0.6 0.0 copy-start
  0.7 0.0 copy-start.1
  0.7 60.5 %shard_map.94 = (bf16[160,512]{1,0:T(8,128)(2,1)}, f32[24,640]{1,0:T(8,128)}, f32[8,128]{1,0:T(8,128)}) custom-call(bf16[160,512]{1,0:T(8,128)(2,1)} %bitcast.7, bf16[1280,640]{1,0:T(8,128)(2,1)} %w_hbm.1, bf16[512,640]{1,0:T(8,128)(2,1)} %h_hbm.1, f32[640]{0:T(1024)} %bias_hbm.1, f32[2]{0:T(128)} %other_hbm.1), custom_call_target="tpu_custom_call" | custom-call | flops 2516582400 | bytes 3145728 | tf_op jit(solution)/shard_map/pallas_call | solution.py:535
  61.2 0.0 copy-done
  61.2 1.5 %add_multiply_fusion = f32[20,640]{1,0:T(8,128)} fusion(f32[20,640]{1,0:T(8,128)S(1)} %copy-done, f32[24,640]{1,0:T(8,128)} %get-tuple-element.7, s32[]{:T(128)S(6)} %select_n.11), kind=kLoop, calls=%fused_computation | loop fusion | flops 25600 | bytes 153604 | tf_op jit(solution)/shard_map/div | solution.py:583
  62.7 0.0 copy-done.1
  62.7 1.3 %fusion = f32[640]{0:T(1024)} fusion(f32[640]{0:T(1024)S(1)} %copy-done.1, f32[8,128]{1,0:T(8,128)} %get-tuple-element.8), kind=kLoop, calls=%fused_computation.2 | loop fusion | flops 1280 | bytes 7680 | tf_op jit(solution)/shard_map/div | solution.py:584
  63.9 1.6 %copy.11 = bf16[512,160]{0,1:T(8,128)(2,1)} copy(bf16[512,160]{0,1:T(8,128)(2,1)} %bitcast.6) | data formatting | bytes 327680
Async XLA Ops:
  0.6 60.5 %copy-start = (f32[20,640]{1,0:T(8,128)S(1)}, f32[20,640]{1,0:T(8,128)}, u32[]{:S(2)}) copy-start(f32[20,640]{1,0:T(8,128)} %param.12) | copy-start | bytes 153604
  0.7 62.0 %copy-start.1 = (f32[640]{0:T(1024)S(1)}, f32[640]{0:T(1024)}, u32[]{:S(2)}) copy-start(f32[640]{0:T(1024)} %param.13) | copy-start | bytes 7684

commit v7 on v6

--- a/solution.py
+++ b/solution.py
@@ -312,7 +312,6 @@
     early(1)
     back_send(0)
     back(1)
-    back_send(1)
     norm_wait(0)
     norm_wait(1)
 
@@ -465,6 +464,7 @@
     bx[px] = f0 * bt[0] + f1 * bt[1]
     for k in range(1, NX):
         start(bx_copy(px, k))
+    back_send(1)
     for way in range(2):
         fy_copy(way).wait_recv()
     for t in range(NB):

time: 65.8 us -> 65.6 us (level)
  no operation moved by 1% of the time
where the time goes in v7:
time: 65.6 us; the launch traced here: 65.4 us
  Pallas kernels  60.3 us (92%)
  other arithmetic  2.75 us (4%)
  local copies, waits for them, and re-layouts  1.6 us (2%)
  between operations  0.68 us (1%)
    pallas_call x1, Pallas kernels, fused(): pl.pallas_call(kernel, out_shape=(jax.ShapeDtypeStruct((R, 2 * SEQ), BF16...  60.3 us
    unnamed x5, local copies, waits for them, and re-layouts  1.6 us
    div x1, other arithmetic, per_device(): weight_grad = (mine + weight_noise) / EXAMPLES  1.47 us

profile of v7, /device:TPU:64, one launch (start us, length us, event | category | flops | bytes accessed | tf_op | source)
XLA Modules:
  0.0 65.4 jit_solution(12629351994299685177)
XLA Ops:
  0.6 0.0 copy-start
  0.7 0.0 copy-start.1
  0.7 60.3 %shard_map.94 = (bf16[160,512]{1,0:T(8,128)(2,1)}, f32[24,640]{1,0:T(8,128)}, f32[8,128]{1,0:T(8,128)}) custom-call(bf16[160,512]{1,0:T(8,128)(2,1)} %bitcast.7, bf16[1280,640]{1,0:T(8,128)(2,1)} %w_hbm.1, bf16[512,640]{1,0:T(8,128)(2,1)} %h_hbm.1, f32[640]{0:T(1024)} %bias_hbm.1, f32[2]{0:T(128)} %other_hbm.1), custom_call_target="tpu_custom_call" | custom-call | flops 2516582400 | bytes 3145728 | tf_op jit(solution)/shard_map/pallas_call | solution.py:535
  61.0 0.0 copy-done
  61.0 1.5 %add_multiply_fusion = f32[20,640]{1,0:T(8,128)} fusion(f32[20,640]{1,0:T(8,128)S(1)} %copy-done, f32[24,640]{1,0:T(8,128)} %get-tuple-element.7, s32[]{:T(128)S(6)} %select_n.11), kind=kLoop, calls=%fused_computation | loop fusion | flops 25600 | bytes 153604 | tf_op jit(solution)/shard_map/div | solution.py:583
  62.5 0.0 copy-done.1
  62.5 1.3 %fusion = f32[640]{0:T(1024)} fusion(f32[640]{0:T(1024)S(1)} %copy-done.1, f32[8,128]{1,0:T(8,128)} %get-tuple-element.8), kind=kLoop, calls=%fused_computation.2 | loop fusion | flops 1280 | bytes 7680 | tf_op jit(solution)/shard_map/div | solution.py:584
  63.8 1.6 %copy.11 = bf16[512,160]{0,1:T(8,128)(2,1)} copy(bf16[512,160]{0,1:T(8,128)(2,1)} %bitcast.6) | data formatting | bytes 327680
Async XLA Ops:
  0.6 60.4 %copy-start = (f32[20,640]{1,0:T(8,128)S(1)}, f32[20,640]{1,0:T(8,128)}, u32[]{:S(2)}) copy-start(f32[20,640]{1,0:T(8,128)} %param.12) | copy-start | bytes 153604
  0.7 61.8 %copy-start.1 = (f32[640]{0:T(1024)S(1)}, f32[640]{0:T(1024)}, u32[]{:S(2)}) copy-start(f32[640]{0:T(1024)} %param.13) | copy-start | bytes 7684
